TPU v7x, 128 devices: a whole 4x4x4 slice. The times are simulated.
128 devices in a mesh: pool: 8 (over y, core), tp: 16 (over z, x).
Axes of the slice: x: 4, y: 4, z: 4, core: 2. Of those that a mesh axis runs over, the one named last changes fastest.
Arguments:
- hidden_in: bfloat16 [2176, 8192], P('pool'), may hold values from -6 to 6
- norm_gain: float32 [8192], replicated, may hold values from 0.1 to 1.9
- w_query: bfloat16 [8192, 4096], P(None, 'tp'), may hold values from -0.0625 to 0.0625
- w_keyval: bfloat16 [8192, 1024], P(None, 'tp'), may hold values from -0.25 to 0.25
- w_out: bfloat16 [4096, 8192], P('tp'), may hold values from -0.09375 to 0.09375
- kv_store: bfloat16 [2048, 4, 2, 128, 128], P(('pool', 'tp')), may hold values from -130 to 130
- page_slots: int32 [8, 128, 3], P(None, ('pool', 'tp')), may hold values from 0 to 15, as said below
- page_counts: int32 [8, 128], P('pool'), may hold values from 1 to 3, 256 in all within a row
Outputs:
- layer_out: bfloat16 [2176, 8192], P('pool', 'tp')
Inputs may be any that keep to these rules, and one draw needn't show every extreme that they name: `page_slots`: the 3 slots of one request and holder are distinct pages. Only slots c < page_counts[r, s] are read. `page_counts`: each row sums to 256; every request has some holder with exactly 3 pages.
All inputs are finite; a program needn't handle non-finite values.
Results may differ from a plain program's by a relative error of at most 0.02.
The roundings to bfloat16 on the way count: a program that leaves them out, or rounds other values in their place, can miss the bound.
Values may be sent and summed in bfloat16 or wider, within the bound.
A program may use at most 192 MiB of HBM per device.

v0:
```python
import math

import jax
import jax.numpy as jnp
from jax import lax
from jax.sharding import PartitionSpec as P

SAMP = 16


def rms_norm(hidden_in, norm_gain):
    as_float = hidden_in.astype(jnp.float32)
    inverse = lax.rsqrt(jnp.mean(as_float * as_float, axis=-1, keepdims=True) + 1e-05)
    return (as_float * inverse * norm_gain).astype(jnp.bfloat16)


def allowed_pairs(row_count, turn_len):
    query_idx = jnp.arange(row_count, dtype=jnp.int32)[:, None]
    key_idx = jnp.arange(row_count, dtype=jnp.int32)[None, :]
    return (key_idx <= query_idx) & ((key_idx < turn_len) | (key_idx == query_idx))


def block_step(carry, query_block, key_block, value_block, key_mask, score_scale):
    running_max, weight_sum, blended = carry
    scores = (
        jnp.einsum("kgre,kne->kgrn", query_block, key_block, preferred_element_type=jnp.float32)
        * score_scale
    )
    scores = jnp.where(key_mask, scores, -jnp.inf)
    new_max = jnp.maximum(running_max, jnp.max(scores, axis=-1))
    shrink = jnp.exp(running_max - new_max)
    probs = jnp.exp(scores - new_max[..., None])
    weight_sum = weight_sum * shrink + jnp.sum(probs, axis=-1)
    blended = blended * shrink[..., None] + jnp.einsum(
        "kgrn,kne->kgre",
        probs.astype(jnp.bfloat16),
        value_block,
        preferred_element_type=jnp.float32,
    )
    return (new_max, weight_sum, blended)


def merge_parts(first_part, second_part):
    joint_max = jnp.maximum(first_part[0], second_part[0])
    first_scale = jnp.exp(first_part[0] - joint_max)
    second_scale = jnp.exp(second_part[0] - joint_max)
    weight_sum = first_part[1] * first_scale + second_part[1] * second_scale
    blended = first_part[2] * first_scale[..., None] + second_part[2] * second_scale[..., None]
    return (joint_max, weight_sum, blended)


def empty_part(kv_count, group_size, row_count, head_size):
    return (
        jnp.full((kv_count, group_size, row_count), -jnp.inf, jnp.float32),
        jnp.zeros((kv_count, group_size, row_count), jnp.float32),
        jnp.zeros((kv_count, group_size, row_count, head_size), jnp.float32),
    )


def local(hidden_in, norm_gain, w_query, w_keyval, w_out, kv_store, page_slots, page_counts):
    row_count, model_width = hidden_in.shape
    kv_heads = kv_store.shape[1]
    page_len = kv_store.shape[3]
    head_size = kv_store.shape[4]
    slot_cap = page_slots.shape[2]
    local_heads = w_query.shape[1] // head_size
    tp_count = lax.axis_size("tp")
    pool_count = lax.axis_size("pool")
    tp_rank = lax.axis_index("tp")
    ranks_per_kv = tp_count // kv_heads
    turn_len = row_count - SAMP
    score_scale = 1.0 / math.sqrt(head_size)
    normed = rms_norm(hidden_in, norm_gain)
    queries = jnp.dot(normed, w_query, preferred_element_type=jnp.float32).astype(jnp.bfloat16)
    kv_piece = jnp.dot(normed, w_keyval, preferred_element_type=jnp.float32).astype(jnp.bfloat16)
    turn_kv = lax.all_gather(kv_piece, "tp", axis=1, tiled=True).reshape(
        row_count, 2, kv_heads, head_size
    )
    own_kv = tp_rank // ranks_per_kv
    local_keys = lax.dynamic_index_in_dim(turn_kv[:, 0], own_kv, 1, keepdims=False)
    local_values = lax.dynamic_index_in_dim(turn_kv[:, 1], own_kv, 1, keepdims=False)
    own_queries = queries.reshape(row_count, local_heads, head_size).transpose(1, 0, 2)[None]
    allowed = allowed_pairs(row_count, turn_len)
    local_part = block_step(
        empty_part(1, local_heads, row_count, head_size),
        own_queries,
        local_keys[None],
        local_values[None],
        allowed[None, None],
        score_scale,
    )
    counts = page_counts[0]
    slot_ids = page_slots[:, 0, :]
    head_of_rank = jnp.arange(tp_count, dtype=jnp.int32) // ranks_per_kv
    held_pages = kv_store[slot_ids[:, None, :], head_of_rank[None, :, None]]
    arrived_pages = lax.all_to_all(
        held_pages.reshape(pool_count * tp_count, slot_cap, 2, page_len, head_size),
        ("pool", "tp"),
        split_axis=0,
        concat_axis=0,
        tiled=True,
    )
    live_slots = (jnp.arange(slot_cap, dtype=jnp.int32)[None, :] < counts[:, None]).reshape(
        pool_count, tp_count * slot_cap
    )
    page_groups = arrived_pages.reshape(pool_count, tp_count * slot_cap, 2, page_len, head_size)

    def visit_block(carry, block_data):
        page_block, live_block = block_data
        key_block = page_block[:, 0].reshape(1, -1, head_size)
        value_block = page_block[:, 1].reshape(1, -1, head_size)
        key_mask = jnp.repeat(live_block, page_len)[None, None, None, :]
        return (block_step(carry, own_queries, key_block, value_block, key_mask, score_scale), None)

    starting = empty_part(1, local_heads, row_count, head_size)
    prefix_part, _ = lax.scan(visit_block, starting, (page_groups, live_slots))
    joint_max, weight_sum, blended = merge_parts(prefix_part, local_part)
    attended = (blended / weight_sum[..., None]).astype(jnp.bfloat16)[0]
    attended = attended.transpose(1, 0, 2).reshape(row_count, local_heads * head_size)
    summed = lax.psum_scatter(
        lax.dot_general(
            w_out, attended, (((0,), (1,)), ((), ())), preferred_element_type=jnp.float32
        ).astype(jnp.bfloat16),
        "tp",
        scatter_dimension=0,
        tiled=True,
    ).astype(jnp.float32)
    return summed.T.astype(jnp.bfloat16)


def solution(mesh):
    return jax.shard_map(
        local,
        mesh=mesh,
        in_specs=(
            P("pool", None),
            P(),
            P(None, "tp"),
            P(None, "tp"),
            P("tp", None),
            P(("pool", "tp"), None, None, None, None),
            P(None, ("pool", "tp"), None),
            P("pool", None),
        ),
        out_specs=P("pool", "tp"),
        check_vma=False,
    )
```

profile of v0, /device:TPU:1, one launch (start us, length us, event | category | flops | bytes accessed | tf_op | source)
XLA Modules:
  0.0 723.0 jit_solution(5088694806241071290)
XLA Ops:
  7.7 19.8 %gather_fusion = bf16[384,2,128,128]{3,2,1,0:T(8,128)(2,1)} fusion(bf16[16,4,2,128,128]{4,3,2,1,0:T(8,128)(2,1)} %param.15, s32[384]{0:T(512)S(1)} %reshape.204), kind=kCustom, calls=%fused_computation | custom fusion | bytes 50334720 | tf_op jit(solution)/shard_map/gather | solution.py:95
  27.5 11.9 %all-to-all-start = ((bf16[128,3,2,128,128]{4,3,2,1,0:T(8,128)(2,1)}), bf16[128,3,2,128,128]{4,3,2,1,0:T(8,128)(2,1)}, u32[]{:S(2)}, u32[]{:S(2)}) async-start(bf16[128,3,2,128,128]{4,3,2,1,0:T(8,128)(2,1)} %bitcast.174), calls=%async_computation | async-start | bytes 50331648 | tf_op jit(solution)/shard_map/all_to_all | solution.py:96
  39.5 3.2 fusion.18
  42.8 4.9 fusion.34
  49.4 4.0 fusion.38
  53.4 394.3 %all_gather.3 = bf16[272,1024]{0,1:T(8,128)(2,1)S(1)} all-gather(bf16[272,64]{0,1:T(8,128)(2,1)S(1)} %fusion.38), channel_id=1, replica_groups=mesh['pool'=8,'tp'=16] {'tp'}, dimensions={1}, use_global_device_ids=true | all-gather | bytes 591872 | tf_op jit(solution)/shard_map/all_gather | solution.py:76
  449.9 171.9 %while.15 = (s32[]{:T(128)}, f32[1,2,272]{2,1,0:T(2,128)S(1)}, f32[1,2,272]{2,1,0:T(2,128)S(1)}, f32[1,2,272,128]{3,2,1,0:T(8,128)}, pred[8,48]{1,0:T(8,128)(4,1...) while((s32[]{:T(128)}, f32[1,2,272]{2,1,0:T(2,128)S(1)}, ...), condition=%wide.region_4.5_spmd.clone, body=%wide.region_1.4_spmd.clone.sunk | while | flops 1748253952 | bytes 112298840 | solution.py:116
  452.7 6.9 bitcast_reduce_fusion.2
  459.6 7.4 %fusion.90 = f32[1,2,272,128]{3,2,1,0:T(8,128)S(1)} fusion(bf16[6144,128,1]{1,0,2:T(8,128)(2,1)S(1)} %bitcast.175, f32[6144,2,272]{0,2,1:T(8,128)} %get-tuple-element.157, f32[2,272]{1,0:T(2,128)S(1)} %bitcast.178, pred[6144]{0:T(1024)(128)(4,1)S(1)} %broadcast_bitcast_fusion.2, f32[1,2,272,128]{3,2,1,0:T(8,128)S(1)} %copy-done.6, ...), kind=kOutput, calls=%fused_computation.11.clone.1 | convolution fusion | flops 869216256 | bytes 15509761 | tf_op jit(solution)/shard_map/while/body/eval_jaxpr/kgrn,kne->kgre/dot_general | solution.py:34
  468.2 3.1 fusion.89
  474.1 6.9 bitcast_reduce_fusion.2
  481.1 7.4 %fusion.90 = f32[1,2,272,128]{3,2,1,0:T(8,128)S(1)} fusion(bf16[6144,128,1]{1,0,2:T(8,128)(2,1)S(1)} %bitcast.175, f32[6144,2,272]{0,2,1:T(8,128)} %get-tuple-element.157, f32[2,272]{1,0:T(2,128)S(1)} %bitcast.178, pred[6144]{0:T(1024)(128)(4,1)S(1)} %broadcast_bitcast_fusion.2, f32[1,2,272,128]{3,2,1,0:T(8,128)S(1)} %copy-done.6, ...), kind=kOutput, calls=%fused_computation.11.clone.1 | convolution fusion | flops 869216256 | bytes 15509761 | tf_op jit(solution)/shard_map/while/body/eval_jaxpr/kgrn,kne->kgre/dot_general | solution.py:34
  489.7 3.1 fusion.89
  495.6 6.9 bitcast_reduce_fusion.2
  502.6 7.4 %fusion.90 = f32[1,2,272,128]{3,2,1,0:T(8,128)S(1)} fusion(bf16[6144,128,1]{1,0,2:T(8,128)(2,1)S(1)} %bitcast.175, f32[6144,2,272]{0,2,1:T(8,128)} %get-tuple-element.157, f32[2,272]{1,0:T(2,128)S(1)} %bitcast.178, pred[6144]{0:T(1024)(128)(4,1)S(1)} %broadcast_bitcast_fusion.2, f32[1,2,272,128]{3,2,1,0:T(8,128)S(1)} %copy-done.6, ...), kind=kOutput, calls=%fused_computation.11.clone.1 | convolution fusion | flops 869216256 | bytes 15509761 | tf_op jit(solution)/shard_map/while/body/eval_jaxpr/kgrn,kne->kgre/dot_general | solution.py:34
  511.2 3.1 fusion.89
  517.1 6.9 bitcast_reduce_fusion.2
  524.1 7.4 %fusion.90 = f32[1,2,272,128]{3,2,1,0:T(8,128)S(1)} fusion(bf16[6144,128,1]{1,0,2:T(8,128)(2,1)S(1)} %bitcast.175, f32[6144,2,272]{0,2,1:T(8,128)} %get-tuple-element.157, f32[2,272]{1,0:T(2,128)S(1)} %bitcast.178, pred[6144]{0:T(1024)(128)(4,1)S(1)} %broadcast_bitcast_fusion.2, f32[1,2,272,128]{3,2,1,0:T(8,128)S(1)} %copy-done.6, ...), kind=kOutput, calls=%fused_computation.11.clone.1 | convolution fusion | flops 869216256 | bytes 15509761 | tf_op jit(solution)/shard_map/while/body/eval_jaxpr/kgrn,kne->kgre/dot_general | solution.py:34
  532.7 3.1 fusion.89
  538.6 6.9 bitcast_reduce_fusion.2
  545.6 7.4 %fusion.90 = f32[1,2,272,128]{3,2,1,0:T(8,128)S(1)} fusion(bf16[6144,128,1]{1,0,2:T(8,128)(2,1)S(1)} %bitcast.175, f32[6144,2,272]{0,2,1:T(8,128)} %get-tuple-element.157, f32[2,272]{1,0:T(2,128)S(1)} %bitcast.178, pred[6144]{0:T(1024)(128)(4,1)S(1)} %broadcast_bitcast_fusion.2, f32[1,2,272,128]{3,2,1,0:T(8,128)S(1)} %copy-done.6, ...), kind=kOutput, calls=%fused_computation.11.clone.1 | convolution fusion | flops 869216256 | bytes 15509761 | tf_op jit(solution)/shard_map/while/body/eval_jaxpr/kgrn,kne->kgre/dot_general | solution.py:34
  554.2 3.1 fusion.89
  560.1 6.9 bitcast_reduce_fusion.2
  567.1 7.4 %fusion.90 = f32[1,2,272,128]{3,2,1,0:T(8,128)S(1)} fusion(bf16[6144,128,1]{1,0,2:T(8,128)(2,1)S(1)} %bitcast.175, f32[6144,2,272]{0,2,1:T(8,128)} %get-tuple-element.157, f32[2,272]{1,0:T(2,128)S(1)} %bitcast.178, pred[6144]{0:T(1024)(128)(4,1)S(1)} %broadcast_bitcast_fusion.2, f32[1,2,272,128]{3,2,1,0:T(8,128)S(1)} %copy-done.6, ...), kind=kOutput, calls=%fused_computation.11.clone.1 | convolution fusion | flops 869216256 | bytes 15509761 | tf_op jit(solution)/shard_map/while/body/eval_jaxpr/kgrn,kne->kgre/dot_general | solution.py:34
  575.7 3.1 fusion.89
  581.6 6.9 bitcast_reduce_fusion.2
  588.6 7.4 %fusion.90 = f32[1,2,272,128]{3,2,1,0:T(8,128)S(1)} fusion(bf16[6144,128,1]{1,0,2:T(8,128)(2,1)S(1)} %bitcast.175, f32[6144,2,272]{0,2,1:T(8,128)} %get-tuple-element.157, f32[2,272]{1,0:T(2,128)S(1)} %bitcast.178, pred[6144]{0:T(1024)(128)(4,1)S(1)} %broadcast_bitcast_fusion.2, f32[1,2,272,128]{3,2,1,0:T(8,128)S(1)} %copy-done.6, ...), kind=kOutput, calls=%fused_computation.11.clone.1 | convolution fusion | flops 869216256 | bytes 15509761 | tf_op jit(solution)/shard_map/while/body/eval_jaxpr/kgrn,kne->kgre/dot_general | solution.py:34
  603.1 6.9 bitcast_reduce_fusion.2
  610.1 7.4 %fusion.90 = f32[1,2,272,128]{3,2,1,0:T(8,128)S(1)} fusion(bf16[6144,128,1]{1,0,2:T(8,128)(2,1)S(1)} %bitcast.175, f32[6144,2,272]{0,2,1:T(8,128)} %get-tuple-element.157, f32[2,272]{1,0:T(2,128)S(1)} %bitcast.178, pred[6144]{0:T(1024)(128)(4,1)S(1)} %broadcast_bitcast_fusion.2, f32[1,2,272,128]{3,2,1,0:T(8,128)S(1)} %copy-done.6, ...), kind=kOutput, calls=%fused_computation.11.clone.1 | convolution fusion | flops 869216256 | bytes 15509761 | tf_op jit(solution)/shard_map/while/body/eval_jaxpr/kgrn,kne->kgre/dot_general | solution.py:34
  618.7 3.1 fusion.89
  623.8 5.6 fusion.17
  629.4 86.8 %reduce-scatter.2.cloned.1.call-done = bf16[512,272]{0,1:T(8,128)(2,1)} async-done(((bf16[8192,272]{0,1:T(8,128)(2,1)}), bf16[512,272]{0,1:T(8,128)(2,1)}) %reduce-scatter.2.cloned.1.call-update) | async-done | bytes 278544 | tf_op jit(solution)/shard_map/reduce_scatter | solution.py:120
  (146 shorter events, 41.5 us)
Async XLA Ops:
  6.5 42.9 %copy-start = (bf16[8192,64]{0,1:T(8,128)(2,1)S(1)}, bf16[8192,64]{0,1:T(8,128)(2,1)}, u32[]{:S(2)}) copy-start(bf16[8192,64]{0,1:T(8,128)(2,1)} %param.13) | copy-start | bytes 3145732
  27.5 15.3 %copy-start.4 = (f32[8192]{0:T(1024)S(1)}, f32[8192]{0:T(1024)}, u32[]{:S(2)}) copy-start(f32[8192]{0:T(1024)} %param.11) | copy-start | bytes 98308
  27.5 421.7 %all-to-all-start = ((bf16[128,3,2,128,128]{4,3,2,1,0:T(8,128)(2,1)}), bf16[128,3,2,128,128]{4,3,2,1,0:T(8,128)(2,1)}, u32[]{:S(2)}, u32[]{:S(2)}) async-start(bf16[128,3,2,128,128]{4,3,2,1,0:T(8,128)(2,1)} %bitcast.174), calls=%async_computation | async-start | bytes 50331648 | tf_op jit(solution)/shard_map/all_to_all | solution.py:96
  39.4 676.8 %reduce-scatter.2.cloned.1.call-start = ((), (), s32[]{:S(2)}) async-start(), calls=%async_computation.2 | async-start | bytes 4734976 | tf_op jit(solution)/shard_map/reduce_scatter | solution.py:120
  42.8 5.5 copy-start.5
  449.0 0.9 copy-start.3
  452.6 7.0 copy-start.6
  459.6 8.6 %copy-start.2 = (f32[6144,2,272]{0,2,1:T(8,128)S(1)}, f32[6144,2,272]{0,2,1:T(8,128)}, u32[]{:S(2)}) copy-start(f32[6144,2,272]{0,2,1:T(8,128)} %get-tuple-element.157) | copy-start | bytes 40108036 | tf_op jit(solution)/shard_map/while
  468.2 3.2 copy-start.7
  474.1 7.0 copy-start.6
  481.1 8.6 %copy-start.2 = (f32[6144,2,272]{0,2,1:T(8,128)S(1)}, f32[6144,2,272]{0,2,1:T(8,128)}, u32[]{:S(2)}) copy-start(f32[6144,2,272]{0,2,1:T(8,128)} %get-tuple-element.157) | copy-start | bytes 40108036 | tf_op jit(solution)/shard_map/while
  489.7 3.2 copy-start.7
  495.6 7.0 copy-start.6
  502.6 8.6 %copy-start.2 = (f32[6144,2,272]{0,2,1:T(8,128)S(1)}, f32[6144,2,272]{0,2,1:T(8,128)}, u32[]{:S(2)}) copy-start(f32[6144,2,272]{0,2,1:T(8,128)} %get-tuple-element.157) | copy-start | bytes 40108036 | tf_op jit(solution)/shard_map/while
  511.2 3.2 copy-start.7
  517.1 7.0 copy-start.6
  524.1 8.6 %copy-start.2 = (f32[6144,2,272]{0,2,1:T(8,128)S(1)}, f32[6144,2,272]{0,2,1:T(8,128)}, u32[]{:S(2)}) copy-start(f32[6144,2,272]{0,2,1:T(8,128)} %get-tuple-element.157) | copy-start | bytes 40108036 | tf_op jit(solution)/shard_map/while
  532.7 3.2 copy-start.7
  538.6 7.0 copy-start.6
  545.6 8.6 %copy-start.2 = (f32[6144,2,272]{0,2,1:T(8,128)S(1)}, f32[6144,2,272]{0,2,1:T(8,128)}, u32[]{:S(2)}) copy-start(f32[6144,2,272]{0,2,1:T(8,128)} %get-tuple-element.157) | copy-start | bytes 40108036 | tf_op jit(solution)/shard_map/while
  554.2 3.2 copy-start.7
  560.1 7.0 copy-start.6
  567.1 8.6 %copy-start.2 = (f32[6144,2,272]{0,2,1:T(8,128)S(1)}, f32[6144,2,272]{0,2,1:T(8,128)}, u32[]{:S(2)}) copy-start(f32[6144,2,272]{0,2,1:T(8,128)} %get-tuple-element.157) | copy-start | bytes 40108036 | tf_op jit(solution)/shard_map/while
  575.7 3.2 copy-start.7
  581.6 7.0 copy-start.6
  588.6 8.6 %copy-start.2 = (f32[6144,2,272]{0,2,1:T(8,128)S(1)}, f32[6144,2,272]{0,2,1:T(8,128)}, u32[]{:S(2)}) copy-start(f32[6144,2,272]{0,2,1:T(8,128)} %get-tuple-element.157) | copy-start | bytes 40108036 | tf_op jit(solution)/shard_map/while
  597.2 3.2 copy-start.7
  603.1 7.0 copy-start.6
  610.1 8.6 %copy-start.2 = (f32[6144,2,272]{0,2,1:T(8,128)S(1)}, f32[6144,2,272]{0,2,1:T(8,128)}, u32[]{:S(2)}) copy-start(f32[6144,2,272]{0,2,1:T(8,128)} %get-tuple-element.157) | copy-start | bytes 40108036 | tf_op jit(solution)/shard_map/while
  618.7 3.2 copy-start.7
  621.9 94.3 %copy-start.1 = (bf16[8192,64]{0,1:T(8,128)(2,1)S(1)}, bf16[8192,64]{0,1:T(8,128)(2,1)}, u32[]{:S(2)}) copy-start(bf16[8192,64]{0,1:T(8,128)(2,1)} %param.13) | copy-start | bytes 3145732
Sparse Core Ops, SparseCore 0:
  629.5 86.6 reduce-scatter.1
where the time goes:
time: 725 us; the launch traced here: 723 us
  blocking collectives  394 us (54%)
  matrix products  131 us (18%)
  waiting for transfers between devices  86.8 us (12%)
  local copies, waits for them, and re-layouts  53.8 us (7%)
  other arithmetic  30.4 us (4%)
  between operations  13.6 us (2%)
  starting transfers between devices  11.9 us (2%)
    all_gather x1, blocking collectives, local(): lax.all_gather(kv_piece, 'tp', axis=1, tiled=True)  394 us
    reduce_scatter x1, waiting for transfers between devices, local(): lax.psum_scatter(lax.dot_general(w_out, attended, (((0,), (1,)), ((), ())...  86.8 us
    dot_general x9, matrix products, block_step(): jnp.einsum('kgrn,kne->kgre', probs.astype(jnp.bfloat16), value_block, pre...  61.1 us
    dot_general x9, matrix products, block_step(): jnp.einsum('kgre,kne->kgrn', query_block, key_block, preferred_element_ty...  55.9 us
    reduce_sum x9, other arithmetic, block_step(): weight_sum = weight_sum * shrink + jnp.sum(probs, axis=-1)  25.2 us
    gather x1, local copies, waits for them, and re-layouts, local(): held_pages = kv_store[slot_ids[:, None, :], head_of_rank[None, :, None]]  19.8 us
    squeeze x16, local copies, waits for them, and re-layouts, local(): prefix_part, _ = lax.scan(visit_block, starting, (page_groups, live_slots))  18.4 us
  transfers between devices with their start and end apart: 2, of which 1 were waited for; matrix products, arithmetic and copies ran while one was open for 2% of the time, Pallas kernels for 0%

commit v1 on v0

v1 whole, which is shorter than its diff:
```python
import math

import jax
import jax.numpy as jnp
from jax import lax
from jax.experimental import pallas as pl
from jax.experimental.pallas import tpu as pltpu
from jax.sharding import PartitionSpec as P

SAMP = 16
MESH = pl.DeviceIdType.MESH
F32 = jnp.float32
BF16 = jnp.bfloat16
PAGE = 128
HD = 128
CAP = 3
LOG2E = 1.4426950408889634
DEAD = 1e30
ROWS = 272
GROUP = 8
QROWS = GROUP * ROWS
BLOCK = 640
QPAD = 4 * BLOCK
TILE = 256
TILES = 9
PARTNERS = 32
CHUNK = 4
NT = (((1,), (1,)), ((), ()))
NN = (((1,), (0,)), ((), ()))


def rms_norm(hidden_in, norm_gain):
    as_float = hidden_in.astype(F32)
    inverse = lax.rsqrt(jnp.mean(as_float * as_float, axis=-1, keepdims=True) + 1e-05)
    return (as_float * inverse * norm_gain).astype(BF16)


def attention_kernel(
    slots_ref, counts_ref, q_ref, turn_ref, kv_ref, out_ref,
    send, recv, qall, acc, stat_m, stat_l, vt, part_out, part_in, lse_out, lse_in,
    kv_ssem, kv_rsem, q_ssem, q_rsem, o_ssem, o_rsem, s_ssem, s_rsem, a_ssem, a_rsem,
):
    pool = lax.axis_index("pool")
    tp = lax.axis_index("tp")
    y, c = pool // 2, pool % 2
    z, x = tp // 4, tp % 4
    scale = LOG2E / math.sqrt(HD)

    def offset_device(i):
        dy, dc, dz = i // 8, (i // 4) % 2, i % 4
        return ((y + dy) % 4) * 2 + (c + dc) % 2, (z + dz) % 4

    def x_peer(d):
        return (pool, z * 4 + (x + d) % 4)

    barrier = pltpu.get_barrier_semaphore()

    def greet(i, carry):
        dest_pool, dest_z = offset_device(i)
        pl.semaphore_signal(barrier, inc=1, device_id=(dest_pool, dest_z * 4 + x), device_id_type=MESH)
        return carry

    lax.fori_loop(1, PARTNERS, greet, 0)
    for d in (1, 2, 3):
        pl.semaphore_signal(barrier, inc=1, device_id=x_peer(d), device_id_type=MESH)

    def fill(i, carry):
        dest_pool, dest_z = offset_device(i)
        for slot in range(CAP):
            page = slots_ref[dest_pool * CAP + slot]
            send[i, slot] = kv_ref[page, dest_z]
        return carry

    for slot in range(CAP):
        recv[0, slot] = kv_ref[slots_ref[pool * CAP + slot], z]
    qall[pl.ds(QROWS, QPAD - QROWS), :] = jnp.zeros((QPAD - QROWS, HD), BF16)
    own_rows = pl.ds(pl.multiple_of(x * 2 * ROWS, 16), 2 * ROWS)
    qall[own_rows, :] = q_ref[...]
    pl.semaphore_wait(barrier, PARTNERS - 1 + 3)

    def q_copy(d):
        return pltpu.make_async_remote_copy(
            src_ref=q_ref, dst_ref=qall.at[own_rows], send_sem=q_ssem.at[d], recv_sem=q_rsem.at[d],
            device_id=x_peer(d), device_id_type=MESH)

    def kv_copy(i):
        dest_pool, dest_z = offset_device(i)
        return pltpu.make_async_remote_copy(
            src_ref=send.at[i], dst_ref=recv.at[i], send_sem=kv_ssem.at[i], recv_sem=kv_rsem.at[i],
            device_id=(dest_pool, dest_z * 4 + x), device_id_type=MESH)

    for d in (1, 2, 3):
        q_copy(d).start()

    def fill_send(i, carry):
        fill(i, carry)
        kv_copy(i).start()
        return carry

    lax.fori_loop(1, PARTNERS, fill_send, 0)

    acc[...] = jnp.zeros_like(acc)
    stat_m[...] = jnp.full_like(stat_m, -DEAD)
    stat_l[...] = jnp.zeros_like(stat_l)
    for d in (1, 2, 3):
        q_copy(d).wait()

    def visit(g, carry):
        @pl.loop(0, CHUNK)
        def _(k):
            @pl.when(g * CHUNK + k > 0)
            def _():
                kv_copy(g * CHUNK + k).wait_recv()

        live = []
        for k in range(CHUNK):
            i = g * CHUNK + k
            dy, dc, dz = i // 8, (i // 4) % 2, i % 4
            holder = (((y + 4 - dy) % 4) * 2 + (c + dc) % 2) * 16 + ((z + 4 - dz) % 4) * 4 + x
            count = counts_ref[holder]
            for slot in range(CAP):
                live.append(count > slot)
        pages = recv[pl.ds(g * CHUNK, CHUNK)]
        keys = pages[:, :, :PAGE, :].reshape(CHUNK * CAP * PAGE, HD)
        vt[...] = pages[:, :, PAGE:, :].reshape(CHUNK * CAP * PAGE, HD).T

        @pl.loop(0, TILES)
        def _(t):
            cols = pl.ds(pl.multiple_of(t * TILE, TILE), TILE)
            scores = lax.dot_general(keys, qall[cols, :], NT, preferred_element_type=F32)
            old_m = stat_m[:, cols]
            new_m = old_m
            for n in range(CHUNK * CAP):
                top = jnp.max(scores[n * PAGE:(n + 1) * PAGE], axis=0, keepdims=True)
                new_m = jnp.maximum(new_m, jnp.where(live[n], top, -DEAD))
            shift = new_m * scale
            total = stat_l[:, cols] * jnp.exp2(old_m * scale - shift)
            weights = []
            for n in range(CHUNK * CAP):
                probs = jnp.exp2(scores[n * PAGE:(n + 1) * PAGE] * scale - jnp.where(live[n], shift, DEAD))
                total = total + jnp.sum(probs, axis=0, keepdims=True)
                weights.append(probs.astype(BF16))
            blended = lax.dot_general(vt[...], jnp.concatenate(weights, axis=0), NN, preferred_element_type=F32)
            acc[:, cols] = acc[:, cols] * jnp.exp2(old_m * scale - shift) + blended
            stat_m[:, cols] = new_m
            stat_l[:, cols] = total

        return carry

    lax.fori_loop(0, PARTNERS // CHUNK, visit, 0)

    block = pl.ds(pl.multiple_of(x * BLOCK, 128), BLOCK)
    own_q = qall[pl.ds(pl.multiple_of(x * BLOCK, 128), BLOCK), :]
    turn_scores = lax.dot_general(turn_ref[0], own_q, NT, preferred_element_type=F32)
    key_idx = lax.broadcasted_iota(jnp.int32, (ROWS, BLOCK), 0)
    row_idx = (lax.broadcasted_iota(jnp.int32, (ROWS, BLOCK), 1) + x * BLOCK) % ROWS
    allowed = (key_idx <= row_idx) & ((key_idx < ROWS - SAMP) | (key_idx == row_idx))
    turn_scores = jnp.where(allowed, turn_scores, -DEAD)
    turn_m = jnp.max(turn_scores, axis=0, keepdims=True)
    turn_p = jnp.exp2(turn_scores * scale - turn_m * scale)
    turn_l = jnp.sum(turn_p, axis=0, keepdims=True)
    turn_o = lax.dot_general(turn_ref[1].T, turn_p.astype(BF16), NN, preferred_element_type=F32)
    turn_lse = turn_m * scale + jnp.log2(turn_l)

    def o_copy(d):
        return pltpu.make_async_remote_copy(
            src_ref=part_out.at[d], dst_ref=part_in.at[d], send_sem=o_ssem.at[d], recv_sem=o_rsem.at[d],
            device_id=x_peer(d), device_id_type=MESH)

    def s_copy(d):
        return pltpu.make_async_remote_copy(
            src_ref=lse_out.at[d], dst_ref=lse_in.at[d], send_sem=s_ssem.at[d], recv_sem=s_rsem.at[d],
            device_id=x_peer(d), device_id_type=MESH)

    for d in (2, 1, 3):
        cols = pl.ds(pl.multiple_of(((x + d) % 4) * BLOCK, 128), BLOCK)
        total = jnp.maximum(stat_l[:, cols], 1e-30)
        part_out[d] = (acc[:, cols] / total).astype(BF16)
        lse_out[d] = jnp.broadcast_to(stat_m[:, cols] * scale + jnp.log2(total), (8, BLOCK))
        o_copy(d).start()
        s_copy(d).start()

    own_l = jnp.maximum(stat_l[:, block], 1e-30)
    own_lse = stat_m[:, block] * scale + jnp.log2(own_l)
    for d in (1, 2, 3):
        o_copy(d).wait()
        s_copy(d).wait()
    lses = [lse_in[d][:1] for d in (1, 2, 3)]
    top = jnp.maximum(own_lse, turn_lse)
    for lse in lses:
        top = jnp.maximum(top, lse)
    own_w = jnp.exp2(own_lse - top)
    turn_w = jnp.exp2(turn_lse - top)
    norm = own_w + turn_w
    merged = acc[:, block] * (own_w / own_l) + turn_o * (turn_w / turn_l)
    for d in (1, 2, 3):
        w = jnp.exp2(lses[d - 1] - top)
        norm = norm + w
        merged = merged + part_in[d].astype(F32) * w
    attended = (merged / norm).T.astype(BF16)

    part_rows = pl.ds(pl.multiple_of(x * BLOCK, 128), BLOCK)
    qall[part_rows, :] = attended

    def a_copy(d):
        return pltpu.make_async_remote_copy(
            src_ref=qall.at[part_rows], dst_ref=out_ref.at[part_rows], send_sem=a_ssem.at[d],
            recv_sem=a_rsem.at[d], device_id=x_peer(d), device_id_type=MESH)

    for d in (2, 1, 3):
        a_copy(d).start()
    out_ref[part_rows, :] = attended
    for d in (1, 2, 3):
        a_copy(d).wait()

    @pl.loop(1, PARTNERS)
    def _(i):
        kv_copy(i).wait_send()


def attend(slots, counts, q, turn, kv):
    vmem = pl.BlockSpec(memory_space=pltpu.VMEM)
    smem = pl.BlockSpec(memory_space=pltpu.SMEM)
    dma = pltpu.SemaphoreType.DMA
    return pl.pallas_call(
        attention_kernel,
        out_shape=jax.ShapeDtypeStruct((QPAD, HD), BF16),
        in_specs=[smem, smem, vmem, vmem, vmem],
        out_specs=vmem,
        scratch_shapes=[
            pltpu.VMEM((PARTNERS, CAP, 2 * PAGE, HD), BF16),
            pltpu.VMEM((PARTNERS, CAP, 2 * PAGE, HD), BF16),
            pltpu.VMEM((QPAD, HD), BF16),
            pltpu.VMEM((HD, QPAD), F32),
            pltpu.VMEM((1, QPAD), F32),
            pltpu.VMEM((1, QPAD), F32),
            pltpu.VMEM((HD, CHUNK * CAP * PAGE), BF16),
            pltpu.VMEM((4, HD, BLOCK), BF16),
            pltpu.VMEM((4, HD, BLOCK), BF16),
            pltpu.VMEM((4, 8, BLOCK), F32),
            pltpu.VMEM((4, 8, BLOCK), F32),
            dma((PARTNERS,)), dma((PARTNERS,)),
            dma((4,)), dma((4,)), dma((4,)), dma((4,)), dma((4,)), dma((4,)), dma((4,)), dma((4,)),
        ],
        compiler_params=pltpu.CompilerParams(
            collective_id=1, has_side_effects=True, vmem_limit_bytes=56 * 2**20),
        cost_estimate=pl.CostEstimate(flops=14 * 10**9, bytes_accessed=8 * 10**6, transcendentals=27 * 10**6),
        name="attend",
    )(slots, counts, q, turn, kv)


def local(hidden_in, norm_gain, w_query, w_keyval, w_out, kv_store, page_slots, page_counts):
    row_count = hidden_in.shape[0]
    tp_rank = lax.axis_index("tp")
    z, x = tp_rank // 4, tp_rank % 4
    normed = rms_norm(hidden_in, norm_gain)
    queries = jnp.dot(normed, w_query, preferred_element_type=F32).astype(BF16)
    kv_piece = jnp.dot(normed, w_keyval, preferred_element_type=F32).astype(BF16)
    turn_kv = lax.all_gather(kv_piece, "tp", axis=1, tiled=True).reshape(row_count, 2, 4, HD)
    turn = lax.dynamic_index_in_dim(turn_kv, z, 2, keepdims=False).transpose(1, 0, 2)
    q = queries.reshape(row_count, 2, HD).transpose(1, 0, 2).reshape(2 * row_count, HD)
    everything = attend(
        page_slots.reshape(-1), page_counts.reshape(-1), q, turn,
        kv_store.reshape(16, 4, 2 * PAGE, HD))
    attended = lax.dynamic_slice_in_dim(everything, x * 2 * ROWS, 2 * ROWS, 0)
    attended = attended.reshape(2, ROWS, HD).transpose(1, 0, 2).reshape(ROWS, 2 * HD)
    summed = lax.psum_scatter(
        lax.dot_general(
            w_out, attended, (((0,), (1,)), ((), ())), preferred_element_type=F32
        ).astype(BF16),
        "tp",
        scatter_dimension=0,
        tiled=True,
    ).astype(F32)
    return summed.T.astype(BF16)


def solution(mesh):
    return jax.shard_map(
        local,
        mesh=mesh,
        in_specs=(
            P("pool", None),
            P(),
            P(None, "tp"),
            P(None, "tp"),
            P("tp", None),
            P(("pool", "tp"), None, None, None, None),
            P(None, ("pool", "tp"), None),
            P("pool", None),
        ),
        out_specs=P("pool", "tp"),
        check_vma=False,
    )
```

time: 725 us -> 294 us (0.41)
  blocking collectives: 394 us -> 21.3 us
  Pallas kernels: 0 us -> 157 us
  matrix products: 131 us -> 8.92 us
  local copies, waits for them, and re-layouts: 53.8 us -> 3.79 us
  other arithmetic: 30.4 us -> 3.33 us
  starting transfers between devices: 11.9 us -> 0.01 us
    all_gather x1, blocking collectives: 394 us -> 21.3 us  [local(): lax.all_gather(kv_piece, 'tp', axis=1, tiled=True)]
    pallas_call x0 -> x1, Pallas kernels: none -> 157 us  [attend(): pl.pallas_call(attention_kernel, out_shape=jax.ShapeDtypeStruct((QPAD, HD...]
    dot_general x20 -> x2, matrix products: 126 us -> 5.57 us  [the longest x1 4.13 us: local(): jnp.dot(normed, w_keyval, preferred_element_type=F32).astype(BF16)]
    reduce_sum x9 -> x0, other arithmetic: 25.2 us -> none  [block_step(): weight_sum = weight_sum * shrink + jnp.sum(probs, axis=-1)]
    gather x1 -> x0, local copies, waits for them, and re-layouts: 19.8 us -> none  [local(): held_pages = kv_store[slot_ids[:, None, :], head_of_rank[None, :, None]]]
    squeeze x16 -> x0, local copies, waits for them, and re-layouts: 18.4 us -> none  [local(): prefix_part, _ = lax.scan(visit_block, starting, (page_groups, live_slots))]
    all_to_all x1 -> x0, starting transfers between devices: 11.9 us -> none  [local(): lax.all_to_all(held_pages.reshape(pool_count * tp_count, slot_cap, 2, pag...]
    while x56 -> x0, local copies, waits for them, and re-layouts: 9.64 us -> none
  transfers between devices with their start and end apart: 2 -> 1, of which waited for: 1 -> 1; matrix products, arithmetic and copies ran while one was open for 2% -> 0% of each run, Pallas kernels for 0% -> 0%
where the time goes in v1:
time: 294 us; the launch traced here: 293 us
  Pallas kernels  157 us (53%)
  waiting for transfers between devices  84.6 us (29%)
  blocking collectives  21.3 us (7%)
  between operations  13.5 us (5%)
  matrix products  8.92 us (3%)
  local copies, waits for them, and re-layouts  3.79 us (1%)
  other arithmetic  3.33 us (1%)
    pallas_call x1, Pallas kernels, attend(): pl.pallas_call(attention_kernel, out_shape=jax.ShapeDtypeStruct((QPAD, HD...  157 us
    reduce_scatter x1, waiting for transfers between devices, local(): lax.psum_scatter(lax.dot_general(w_out, attended, (((0,), (1,)), ((), ())...  84.6 us
    all_gather x1, blocking collectives, local(): lax.all_gather(kv_piece, 'tp', axis=1, tiled=True)  21.3 us
  transfers between devices with their start and end apart: 1, of which 1 were waited for; matrix products, arithmetic and copies ran while one was open for 0% of the time, Pallas kernels for 0%

profile of v1, /device:TPU:1, one launch (start us, length us, event | category | flops | bytes accessed | tf_op | source)
XLA Modules:
  0.0 292.7 jit_solution(3940585547156617317)
XLA Ops:
  6.5 0.0 copy-start
  6.5 0.0 copy-start.2
  6.5 0.0 copy-start.4
  6.5 0.0 reduce-scatter.2.cloned.1.call-start
  6.6 0.0 slice-start
  6.6 3.3 %fusion.1 = f32[272]{0:T(512)S(1)} fusion(bf16[272,8192]{1,0:T(8,128)(2,1)} %param.8), kind=kLoop, calls=%fused_computation.4 | loop fusion | flops 6684400 | bytes 4457536 | tf_op jit(solution)/shard_map/reduce_sum | solution.py:34
  9.9 0.0 copy-done.2
  9.9 0.1 copy.15
  10.0 0.6 reshape.33.slots_ref
  10.6 0.0 copy-done
  10.6 0.0 copy-done.4
  10.6 0.0 slice-start.1
  10.6 0.0 copy-start.3
  10.6 4.1 %fusion.14 = bf16[272,64]{0,1:T(8,128)(2,1)S(1)} fusion(bf16[8192,64]{0,1:T(8,128)(2,1)S(1)} %copy-done, bf16[272,8192]{1,0:T(8,128)(2,1)} %param.8, f32[8192]{0:T(1024)S(1)} %copy-done.4, f32[272]{0:T(512)S(1)} %add_rsqrt_fusion), kind=kOutput, calls=%fused_computation.11 | convolution fusion | flops 294142976 | bytes 5573696 | tf_op jit(solution)/shard_map/dot_general | solution.py:258
  14.8 0.0 slice-done
  14.8 0.0 slice-done.1
  14.8 0.6 copy-done.3
  15.4 1.4 fusion.11
  16.9 0.7 copy.27
  17.6 21.3 %all_gather.3 = bf16[272,1024]{0,1:T(8,128)(2,1)S(1)} all-gather(bf16[272,64]{0,1:T(8,128)(2,1)S(1)} %fusion.14), channel_id=1, replica_groups=mesh['pool'=8,'tp'=16] {'tp'}, dimensions={1}, use_global_device_ids=true | all-gather | bytes 591872 | tf_op jit(solution)/shard_map/all_gather | solution.py:259
  38.9 0.8 copy.19
  39.7 0.0 copy-start.1
  39.7 157.2 %attend.1 = bf16[2560,128]{1,0:T(8,128)(2,1)} custom-call(s32[24]{0:T(128)} %reshape.33.slots_ref, s32[128]{0:T(128)} %bitcast.36, bf16[544,128]{1,0:T(8,128)(2,1)} %bitcast.33, bf16[2,272,128]{2,1,0:T(8,128)(2,1)} %bitcast.34, bf16[16,4,256,128]{3,2,1,0:T(8,128)(2,1)} %bitcast.35), custom_call_target="tpu_custom_call" | custom-call | flops 14000000000 | bytes 8000000 | tf_op jit(solution)/shard_map/attend/pallas_call | solution.py:225
  196.9 0.9 constant_dynamic-slice_fusion
  197.9 0.0 copy-done.1
  197.9 3.3 %fusion = bf16[8192,272]{0,1:T(8,128)(2,1)} fusion(bf16[256,8192]{1,0:T(8,128)(2,1)S(1)} %copy-done.1, bf16[2,34,8,128]{3,2,1,0:T(8,128)(2,1)S(1)} %bitcast.32), kind=kOutput, calls=%fused_computation.3 | convolution fusion | flops 1143078912 | bytes 8790016 | tf_op jit(solution)/shard_map/dot_general | solution.py:268
  201.2 0.0 reduce-scatter.2.cloned.1.call-update
  201.2 84.6 %reduce-scatter.2.cloned.1.call-done = bf16[512,272]{0,1:T(8,128)(2,1)} async-done(((bf16[8192,272]{0,1:T(8,128)(2,1)}), bf16[512,272]{0,1:T(8,128)(2,1)}) %reduce-scatter.2.cloned.1.call-update) | async-done | bytes 278544 | tf_op jit(solution)/shard_map/reduce_scatter | solution.py:267
  (3 shorter events, 0.0 us)
Async XLA Ops:
  6.5 4.1 %copy-start = (bf16[8192,64]{0,1:T(8,128)(2,1)S(1)}, bf16[8192,64]{0,1:T(8,128)(2,1)}, u32[]{:S(2)}) copy-start(bf16[8192,64]{0,1:T(8,128)(2,1)} %param.11) | copy-start | bytes 3145732
  6.5 3.4 %copy-start.2 = (s32[8,1,3]{0,1,2:T(1,128)S(1)}, s32[8,1,3]{0,1,2:T(1,128)}, u32[]{:S(2)}) copy-start(s32[8,1,3]{0,1,2:T(1,128)} %param.14) | copy-start | bytes 292
  6.5 4.1 %copy-start.4 = (f32[8192]{0:T(1024)S(1)}, f32[8192]{0:T(1024)}, u32[]{:S(2)}) copy-start(f32[8192]{0:T(1024)} %param.9) | copy-start | bytes 98308
  6.5 279.3 %reduce-scatter.2.cloned.1.call-start = ((), (), s32[]{:S(2)}) async-start(), calls=%async_computation.1 | async-start | bytes 4734976 | tf_op jit(solution)/shard_map/reduce_scatter | solution.py:267
  6.6 8.2 %slice-start = ((s8[4456448]{0:T(1024)(128)(4,1)}), s8[262144]{0:T(1024)(128)(4,1)S(1)}, s32[]{:S(2)}) async-start(s8[4456448]{0:T(1024)(128)(4,1)} %bitcast.29), calls=%async_computation.2 | async-start | bytes 524288
  10.6 4.2 %slice-start.1 = ((s8[4456448]{0:T(1024)(128)(4,1)}), s8[4194304]{0:T(1024)(128)(4,1)S(1)}, s32[]{:S(2)}) async-start(s8[4456448]{0:T(1024)(128)(4,1)} %bitcast.29), calls=%async_computation.3 | async-start | bytes 8388608
  10.6 4.8 %copy-start.3 = (bf16[8192,256]{1,0:T(8,128)(2,1)S(1)}, bf16[8192,256]{1,0:T(8,128)(2,1)}, u32[]{:S(2)}) copy-start(bf16[8192,256]{1,0:T(8,128)(2,1)} %param.10) | copy-start | bytes 12582916
  39.7 158.1 %copy-start.1 = (bf16[256,8192]{1,0:T(8,128)(2,1)S(1)}, bf16[256,8192]{1,0:T(8,128)(2,1)}, u32[]{:S(2)}) copy-start(bf16[256,8192]{1,0:T(8,128)(2,1)} %param.12) | copy-start | bytes 12582916
Sparse Core Ops, SparseCore 0:
  201.4 84.4 reduce-scatter.1

commit v2 on v1

v2 whole, which is shorter than its diff:
```python
import math

import jax
import jax.numpy as jnp
from jax import lax
from jax.experimental import pallas as pl
from jax.experimental.pallas import tpu as pltpu
from jax.sharding import PartitionSpec as P

SAMP = 16
MESH = pl.DeviceIdType.MESH
F32 = jnp.float32
BF16 = jnp.bfloat16
PAGE = 128
HD = 128
CAP = 3
D = 8192
LOG2E = 1.4426950408889634
DEAD = 1e30
ROWS = 272
GROUP = 8
QROWS = GROUP * ROWS
BLOCK = 640
QPAD = 4 * BLOCK
TILE = 256
TILES = 9
UNROLL = 3
SOURCES = 8
CHUNK = 4
KEYS = CHUNK * CAP * PAGE
PART = 512
OUT = 512
NT = (((1,), (1,)), ((), ()))
NN = (((1,), (0,)), ((), ()))
FAR_FIRST = (2, 1, 3)


def plane_offset(i):
    dy = jnp.where(i < 2, 0, jnp.where(i < 6, 1 + 2 * (i % 2), 2))
    dc = jnp.where((i >= 2) & (i < 6), (i - 2) // 2, i % 2)
    return dy, dc


def stage_offset(k):
    return jnp.where(k < 2, k, 5 - k)


def layer_kernel(
    slots_ref, counts_ref, gain_ref, hidden_hbm, wq_hbm, wkv_hbm, wout_hbm, kv_hbm, out_ref,
    hidden, wq, wkv, wout, held0, held1, held2, held3, slots_in, slots_smem,
    ysend, yrecv, squares, q_acc, kv_acc, qown, qall, piece, pieces, turn,
    acc, stat_m, stat_l, vt, turn_o, turn_lse,
    part_out, part_in, lse_out, lse_in, att_out, att_all, sum_out, sum_in,
    load_sem, wout_load_sem, slot_sem, zk_s, zk_r, zs_s, zs_r, zp_s, zp_r, y_s, y_r,
    xq_s, xq_r, xt_s, xt_r, xw_s, xw_r, xo_s, xo_r, xl_s, xl_r, xa_s, xa_r, zo_s, zo_r,
):
    pool = lax.axis_index("pool")
    tp = lax.axis_index("tp")
    y, c = pool // 2, pool % 2
    z, x = tp // 4, tp % 4
    scale = LOG2E / math.sqrt(HD)
    held = (held0, held1, held2, held3)

    def x_peer(d):
        return (pool, z * 4 + (x + d) % 4)

    def z_peer(d):
        return (pool, ((z + d) % 4) * 4 + x)

    def plane_peer(i):
        dy, dc = plane_offset(i)
        return ((y + dy) % 4) * 2 + (c + dc) % 2

    def remote(src, dst, send_sem, recv_sem, device):
        return pltpu.make_async_remote_copy(
            src_ref=src, dst_ref=dst, send_sem=send_sem, recv_sem=recv_sem, device_id=device, device_id_type=MESH)

    barrier = pltpu.get_barrier_semaphore()
    for i in range(1, SOURCES):
        pl.semaphore_signal(barrier, inc=1, device_id=(plane_peer(i), tp), device_id_type=MESH)
    for d in (1, 2, 3):
        pl.semaphore_signal(barrier, inc=1, device_id=x_peer(d), device_id_type=MESH)
        pl.semaphore_signal(barrier, inc=1, device_id=z_peer(d), device_id_type=MESH)

    own_pages = pltpu.make_async_copy(kv_hbm.at[:, z], held0, load_sem.at[0])
    own_pages.start()
    loads = [
        pltpu.make_async_copy(hidden_hbm, hidden, load_sem.at[1]),
        pltpu.make_async_copy(wq_hbm, wq, load_sem.at[2]),
        pltpu.make_async_copy(wkv_hbm, wkv, load_sem.at[3]),
    ]
    for load in loads:
        load.start()
    own_slots = pltpu.make_async_copy(slots_ref, slots_smem.at[0], slot_sem.at[0])
    own_slots.start()
    pl.semaphore_wait(barrier, SOURCES - 1 + 6)

    def slot_copy(d):
        return remote(slots_ref, slots_in.at[d], zs_s.at[d], zs_r.at[d], z_peer(d))

    def page_copy(d):
        return remote(kv_hbm.at[:, (z + d) % 4], held[d], zk_s.at[d], zk_r.at[d], z_peer(d))

    for d in (1, 3, 2):
        slot_copy(d).start()
    for d in (1, 3):
        page_copy(d).start()

    def y_copy(k, i):
        return remote(
            ysend.at[k, i], yrecv.at[k, i], y_s.at[k * SOURCES + i], y_r.at[k * SOURCES + i], (plane_peer(i), tp))

    def pass_on(k, d):
        for slot in range(CAP):
            yrecv[k, 0, slot] = held[d][slots_smem[d, pool, slot]]

        @pl.loop(1, SOURCES)
        def _(n):
            i = jnp.where(n < SOURCES - 1, n + 1, 1)
            dest = plane_peer(i)
            for slot in range(CAP):
                ysend[k, i, slot] = held[d][slots_smem[d, dest, slot]]
            y_copy(k, i).start()

    own_slots.wait()
    own_pages.wait()
    pass_on(0, 0)

    for load in loads:
        load.wait()
    squares[...] = jnp.zeros_like(squares)

    @pl.loop(0, D // PART)
    def _(n):
        part = hidden[:, pl.ds(pl.multiple_of(n * PART, PART), PART)].astype(F32)
        part = part * part
        for m in range(PART // 128):
            squares[...] += part[:, m * 128:(m + 1) * 128]

    mean = jnp.sum(squares[...], axis=1, keepdims=True) * (1.0 / D)
    squares[...] = jnp.broadcast_to(lax.rsqrt(mean + 1e-05), squares.shape)
    q_acc[...] = jnp.zeros_like(q_acc)
    kv_acc[...] = jnp.zeros_like(kv_acc)

    @pl.loop(0, D // PART)
    def _(n):
        cols = pl.ds(pl.multiple_of(n * PART, PART), PART)
        inverse = squares[:, :1]
        normed = (hidden[:, cols].astype(F32) * inverse * gain_ref[:, cols]).astype(BF16)
        q_acc[...] += jnp.dot(normed, wq[cols, :], preferred_element_type=F32)
        kv_acc[...] += lax.dot_general(normed, wkv[:, cols], NT, preferred_element_type=F32)

    queries = q_acc[...].astype(BF16)
    qown[:ROWS, :] = queries[:, :HD]
    qown[ROWS:, :] = queries[:, HD:]
    own_rows = pl.ds(pl.multiple_of(x * 2 * ROWS, 16), 2 * ROWS)

    def q_copy(d):
        return remote(qown, qall.at[own_rows], xq_s.at[d], xq_r.at[d], x_peer(d))

    for d in FAR_FIRST:
        q_copy(d).start()
    qall[own_rows, :] = qown[...]
    qall[pl.ds(QROWS, QPAD - QROWS), :] = jnp.zeros((QPAD - QROWS, HD), BF16)

    half = kv_acc[...]
    blank = jnp.zeros_like(half)
    piece[...] = jnp.where(
        x % 2 == 0, jnp.concatenate([half, blank], axis=1), jnp.concatenate([blank, half], axis=1)).astype(BF16)

    def piece_copy(d):
        return remote(piece, pieces.at[z], zp_s.at[d], zp_r.at[d], z_peer(d))

    for d in (1, 2, 3):
        piece_copy(d).start()
    pieces[z] = piece[...]

    def wout_copy(d, n):
        columns = pl.ds(pl.multiple_of((n * 4 + (x + d) % 4) * OUT, OUT), OUT)
        rows = pl.ds(pl.multiple_of(x * 256, 256), 256)
        return remote(wout_hbm.at[:, columns], wout.at[n, rows], xw_s.at[d * 4 + n], xw_r.at[d * 4 + n], x_peer(d))

    def own_wout(n):
        columns = pl.ds(pl.multiple_of((n * 4 + x) * OUT, OUT), OUT)
        rows = pl.ds(pl.multiple_of(x * 256, 256), 256)
        return pltpu.make_async_copy(wout_hbm.at[:, columns], wout.at[n, rows], wout_load_sem.at[n])

    acc[...] = jnp.zeros_like(acc)
    stat_m[...] = jnp.full_like(stat_m, -DEAD)
    stat_l[...] = jnp.zeros_like(stat_l)
    for d in (1, 2, 3):
        q_copy(d).wait()

    def turn_copy(d, kind):
        return remote(
            pieces.at[kind * 2 + z // 2], turn.at[kind, x], xt_s.at[d * 2 + kind], xt_r.at[d * 2 + kind], x_peer(d))

    def arrived(d, k):
        page_copy(d).wait_recv()
        slot_copy(d).wait_recv()
        to_smem = pltpu.make_async_copy(slots_in.at[d], slots_smem.at[d], slot_sem.at[d])
        to_smem.start()
        to_smem.wait()
        pass_on(k, d)

    def visit(n, carry):
        k, first = n // 2, (n % 2) * CHUNK

        @pl.loop(0, CHUNK)
        def _(j):
            @pl.when(first + j > 0)
            def _():
                y_copy(k, first + j).wait_recv()

        live = []
        for j in range(CHUNK):
            dy, dc = plane_offset(first + j)
            holder = (((y + 4 - dy) % 4) * 2 + (c + dc) % 2) * 16 + ((z + 4 - stage_offset(k)) % 4) * 4 + x
            count = counts_ref[holder]
            for slot in range(CAP):
                live.append(count > slot)
        pages = yrecv[k, pl.ds(first, CHUNK)]
        keys = pages[:, :, :PAGE, :].reshape(KEYS, HD)
        vt[...] = pages[:, :, PAGE:, :].reshape(KEYS, HD).T

        @pl.loop(0, TILES // UNROLL)
        def _(t):
            cols = [pl.ds(pl.multiple_of((t * UNROLL + u) * TILE, TILE), TILE) for u in range(UNROLL)]
            all_scores = [
                lax.dot_general(keys, qall[cols[u], :], NT, preferred_element_type=F32) for u in range(UNROLL)]
            for u in range(UNROLL):
                scores = all_scores[u]
                old_m = stat_m[:, cols[u]]
                new_m = old_m
                for j in range(CHUNK * CAP):
                    top = jnp.max(scores[j * PAGE:(j + 1) * PAGE], axis=0, keepdims=True)
                    new_m = jnp.maximum(new_m, jnp.where(live[j], top, -DEAD))
                shift = new_m * scale
                shrink = jnp.exp2(old_m * scale - shift)
                total = stat_l[:, cols[u]] * shrink
                weights = []
                for j in range(CHUNK * CAP):
                    probs = jnp.exp2(scores[j * PAGE:(j + 1) * PAGE] * scale - jnp.where(live[j], shift, DEAD))
                    total = total + jnp.sum(probs, axis=0, keepdims=True)
                    weights.append(probs.astype(BF16))
                blended = lax.dot_general(vt[...], jnp.concatenate(weights, axis=0), NN, preferred_element_type=F32)
                acc[:, cols[u]] = acc[:, cols[u]] * shrink + blended
                stat_m[:, cols[u]] = new_m
                stat_l[:, cols[u]] = total

        @pl.when(n == 0)
        def _():
            arrived(1, 1)
            arrived(3, 2)
            page_copy(2).start()
            for d in (1, 2, 3):
                piece_copy(d).wait()
            for d in FAR_FIRST:
                for kind in range(2):
                    turn_copy(d, kind).start()
            for kind in range(2):
                turn[kind, x] = pieces[kind * 2 + z // 2]
            for d in FAR_FIRST:
                for m in range(4):
                    wout_copy(d, m).start()
            for m in range(4):
                own_wout(m).start()

        @pl.when(n == 3)
        def _():
            arrived(2, 3)

        return carry

    lax.fori_loop(0, 2 * 4, visit, 0)

    for d in (1, 2, 3):
        for kind in range(2):
            turn_copy(d, kind).wait()
    pair = (z % 2) * 2
    turn_k = turn[0, pair] + turn[0, pair + 1]
    turn_v = turn[1, pair] + turn[1, pair + 1]
    block = pl.ds(pl.multiple_of(x * BLOCK, 128), BLOCK)
    turn_scores = lax.dot_general(turn_k, qall[block, :], NT, preferred_element_type=F32)
    key_idx = lax.broadcasted_iota(jnp.int32, (ROWS, BLOCK), 0)
    row_idx = (lax.broadcasted_iota(jnp.int32, (ROWS, BLOCK), 1) + x * BLOCK) % ROWS
    allowed = (key_idx <= row_idx) & ((key_idx < ROWS - SAMP) | (key_idx == row_idx))
    turn_scores = jnp.where(allowed, turn_scores, -DEAD)
    turn_m = jnp.max(turn_scores, axis=0, keepdims=True)
    turn_p = jnp.exp2(turn_scores * scale - turn_m * scale)
    turn_l = jnp.sum(turn_p, axis=0, keepdims=True)
    turn_o[...] = lax.dot_general(turn_v.T, turn_p.astype(BF16), NN, preferred_element_type=F32) / turn_l
    turn_lse[...] = turn_m * scale + jnp.log2(turn_l)

    def o_copy(d):
        return remote(part_out.at[d], part_in.at[d], xo_s.at[d], xo_r.at[d], x_peer(d))

    def l_copy(d):
        return remote(lse_out.at[d], lse_in.at[d], xl_s.at[d], xl_r.at[d], x_peer(d))

    for d in FAR_FIRST:
        cols = pl.ds(pl.multiple_of(((x + d) % 4) * BLOCK, 128), BLOCK)
        total = jnp.maximum(stat_l[:, cols], 1e-30)
        part_out[d] = (acc[:, cols] / total).astype(BF16)
        lse_out[d] = jnp.broadcast_to(stat_m[:, cols] * scale + jnp.log2(total), (8, BLOCK))
        o_copy(d).start()
        l_copy(d).start()

    own_l = jnp.maximum(stat_l[:, block], 1e-30)
    own_lse = stat_m[:, block] * scale + jnp.log2(own_l)
    for d in (1, 2, 3):
        o_copy(d).wait()
        l_copy(d).wait()
    lses = [lse_in[d][:1] for d in (1, 2, 3)]
    top = jnp.maximum(own_lse, turn_lse[...])
    for lse in lses:
        top = jnp.maximum(top, lse)
    own_w = jnp.exp2(own_lse - top)
    turn_w = jnp.exp2(turn_lse[...] - top)
    norm = own_w + turn_w
    merged = acc[:, block] * (own_w / own_l) + turn_o[...] * turn_w
    for d in (1, 2, 3):
        w = jnp.exp2(lses[d - 1] - top)
        norm = norm + w
        merged = merged + part_in[d].astype(F32) * w
    att_out[...] = (merged / norm).T.astype(BF16)

    def a_copy(d):
        return remote(att_out, att_all.at[block], xa_s.at[d], xa_r.at[d], x_peer(d))

    for d in FAR_FIRST:
        a_copy(d).start()
    att_all[block, :] = att_out[...]
    for d in (1, 2, 3):
        for m in range(4):
            wout_copy(d, m).wait()
    for m in range(4):
        own_wout(m).wait()
    for d in (1, 2, 3):
        a_copy(d).wait()

    attended = jnp.concatenate([att_all[h * ROWS:(h + 1) * ROWS, :] for h in range(GROUP)], axis=1)

    def z_copy(d):
        return remote(sum_out.at[d], sum_in.at[d], zo_s.at[d], zo_r.at[d], z_peer(d))

    for d in FAR_FIRST:
        sum_out[d] = jnp.dot(attended, wout[(z + d) % 4], preferred_element_type=F32).astype(BF16)
        z_copy(d).start()
    result = jnp.dot(attended, wout[z], preferred_element_type=F32)
    for d in (1, 2, 3):
        z_copy(d).wait()
        result = result + sum_in[d].astype(F32)
    out_ref[...] = result.astype(BF16)

    for d in (1, 2, 3):
        page_copy(d).wait_send()
        slot_copy(d).wait_send()

    @pl.loop(0, 4)
    def _(k):
        @pl.loop(1, SOURCES)
        def _(i):
            y_copy(k, i).wait_send()


def local(hidden_in, norm_gain, w_query, w_keyval, w_out, kv_store, page_slots, page_counts):
    vmem = pl.BlockSpec(memory_space=pltpu.VMEM)
    smem = pl.BlockSpec(memory_space=pltpu.SMEM)
    anywhere = pl.BlockSpec(memory_space=pl.ANY)
    dma = pltpu.SemaphoreType.DMA
    slots = jnp.pad(page_slots[:, 0, :], ((0, 0), (0, 128 - CAP)))
    return pl.pallas_call(
        layer_kernel,
        out_shape=jax.ShapeDtypeStruct((ROWS, OUT), BF16),
        in_specs=[vmem, smem, vmem, anywhere, anywhere, anywhere, anywhere, anywhere],
        out_specs=vmem,
        scratch_shapes=[
            pltpu.VMEM((ROWS, D), BF16),
            pltpu.VMEM((D, 256), BF16),
            pltpu.VMEM((64, D), BF16),
            pltpu.VMEM((4, 1024, OUT), BF16),
            pltpu.VMEM((16, 2 * PAGE, HD), BF16),
            pltpu.VMEM((16, 2 * PAGE, HD), BF16),
            pltpu.VMEM((16, 2 * PAGE, HD), BF16),
            pltpu.VMEM((16, 2 * PAGE, HD), BF16),
            pltpu.VMEM((4, 8, 128), jnp.int32),
            pltpu.SMEM((4, 8, 128), jnp.int32),
            pltpu.VMEM((4, SOURCES, CAP, 2 * PAGE, HD), BF16),
            pltpu.VMEM((4, SOURCES, CAP, 2 * PAGE, HD), BF16),
            pltpu.VMEM((ROWS, 128), F32),
            pltpu.VMEM((ROWS, 256), F32),
            pltpu.VMEM((ROWS, 64), F32),
            pltpu.VMEM((2 * ROWS, HD), BF16),
            pltpu.VMEM((QPAD, HD), BF16),
            pltpu.VMEM((ROWS, HD), BF16),
            pltpu.VMEM((4, ROWS, HD), BF16),
            pltpu.VMEM((2, 4, ROWS, HD), BF16),
            pltpu.VMEM((HD, QPAD), F32),
            pltpu.VMEM((1, QPAD), F32),
            pltpu.VMEM((1, QPAD), F32),
            pltpu.VMEM((HD, KEYS), BF16),
            pltpu.VMEM((HD, BLOCK), F32),
            pltpu.VMEM((1, BLOCK), F32),
            pltpu.VMEM((4, HD, BLOCK), BF16),
            pltpu.VMEM((4, HD, BLOCK), BF16),
            pltpu.VMEM((4, 8, BLOCK), F32),
            pltpu.VMEM((4, 8, BLOCK), F32),
            pltpu.VMEM((BLOCK, HD), BF16),
            pltpu.VMEM((QPAD, HD), BF16),
            pltpu.VMEM((4, ROWS, OUT), BF16),
            pltpu.VMEM((4, ROWS, OUT), BF16),
            dma((4,)), dma((4,)), dma((4,)),
            dma((4,)), dma((4,)), dma((4,)), dma((4,)), dma((4,)), dma((4,)),
            dma((4 * SOURCES,)), dma((4 * SOURCES,)),
            dma((4,)), dma((4,)), dma((8,)), dma((8,)), dma((16,)), dma((16,)),
            dma((4,)), dma((4,)), dma((4,)), dma((4,)), dma((4,)), dma((4,)),
            dma((4,)), dma((4,)),
        ],
        compiler_params=pltpu.CompilerParams(
            collective_id=1, has_side_effects=True, vmem_limit_bytes=62 * 2**20),
        cost_estimate=pl.CostEstimate(flops=17 * 10**9, bytes_accessed=19 * 10**6, transcendentals=27 * 10**6),
        name="layer",
    )(
        slots, page_counts.reshape(-1), norm_gain.reshape(1, D), hidden_in, w_query, w_keyval.T, w_out,
        kv_store.reshape(16, 4, 2 * PAGE, HD))


def solution(mesh):
    return jax.shard_map(
        local,
        mesh=mesh,
        in_specs=(
            P("pool", None),
            P(),
            P(None, "tp"),
            P(None, "tp"),
            P("tp", None),
            P(("pool", "tp"), None, None, None, None),
            P(None, ("pool", "tp"), None),
            P("pool", None),
        ),
        out_specs=P("pool", "tp"),
        check_vma=False,
    )
```

time: 294 us -> 131 us (0.45)
  waiting for transfers between devices: 84.6 us -> 0 us
  Pallas kernels: 157 us -> 128 us
  blocking collectives: 21.3 us -> 0 us
  between operations: 13.5 us -> 0.01 us
  matrix products: 8.92 us -> 0 us
  other arithmetic: 3.33 us -> 0 us
    reduce_scatter x1 -> x0, waiting for transfers between devices: 84.6 us -> none  [local(): lax.psum_scatter(lax.dot_general(w_out, attended, (((0,), (1,)), ((), ())...]
    pallas_call x1, Pallas kernels: 157 us -> 128 us  [local(): pl.pallas_call(layer_kernel, out_shape=jax.ShapeDtypeStruct((ROWS, OUT),...]
    all_gather x1 -> x0, blocking collectives: 21.3 us -> none  [local(): lax.all_gather(kv_piece, 'tp', axis=1, tiled=True)]
    dot_general x3 -> x0, matrix products: 8.92 us -> none  [the longest x1 4.13 us: local(): jnp.dot(normed, w_keyval, preferred_element_type=F32).astype(BF16)]
    reduce_sum x1 -> x0, other arithmetic: 3.32 us -> none  [rms_norm(): jnp.mean(as_float * as_float, axis=-1, keepdims=True) + 1e-05]
  transfers between devices with their start and end apart: 1 -> 0, of which waited for: 1 -> 0; matrix products, arithmetic and copies ran while one was open for 0% -> 0% of each run, Pallas kernels for 0% -> 0%
where the time goes in v2:
time: 131 us
  Pallas kernels  128 us (98%)
  local copies, waits for them, and re-layouts  3.04 us (2%)
    pallas_call x1, Pallas kernels, local(): pl.pallas_call(layer_kernel, out_shape=jax.ShapeDtypeStruct((ROWS, OUT),...  128 us

profile of v2, /device:TPU:1, one launch (start us, length us, event | category | flops | bytes accessed | tf_op | source)
XLA Modules:
  0.0 130.6 jit_solution(11896174898168834009)
XLA Ops:
  0.0 0.8 copy.10
  0.8 0.6 pad.4.slots_ref
  1.4 127.6 %layer.1 = bf16[272,512]{1,0:T(8,128)(2,1)} custom-call(s32[8,128]{1,0:T(8,128)} %pad.4.slots_ref, s32[128]{0:T(128)} %bitcast.9, f32[1,8192]{1,0:T(1,128)} %bitcast.8, bf16[272,8192]{1,0:T(8,128)(2,1)} %hidden_hbm.1, bf16[8192,256]{1,0:T(8,128)(2,1)} %wq_hbm.1, bf16[64,8192]{1,0:T(8,128)(2,1)} %bitcast.7, bf16[256,8192]{1,0:T(8,128)(2,1)} %wout_hbm.1, ...), custom_call_target="tpu_custom_call" | custom-call | flops 16999999488 | bytes 19000000 | tf_op jit(solution)/shard_map/layer/pallas_call | solution.py:373
  128.9 1.7 %copy.12 = bf16[272,512]{1,0:T(8,128)(2,1)} copy(bf16[272,512]{1,0:T(8,128)(2,1)} %layer.1) | data formatting | bytes 557056

commit v3 on v2

--- a/solution.py
+++ b/solution.py
@@ -19,14 +19,17 @@
 DEAD = 1e30
 ROWS = 272
 GROUP = 8
+SPAN = 128
+PAIR = 2 * SPAN
+LATE = 144
 QROWS = GROUP * ROWS
-BLOCK = 640
-QPAD = 4 * BLOCK
+QPAD = 2304
 TILE = 256
-TILES = 9
-UNROLL = 3
+FIRST_TILES = (0, 1, 2, 3)
+LATER_TILES = (4, 5, 6, 7, 8)
 SOURCES = 8
 CHUNK = 4
+STEPS = 8
 KEYS = CHUNK * CAP * PAGE
 PART = 512
 OUT = 512
@@ -49,8 +52,9 @@
     slots_ref, counts_ref, gain_ref, hidden_hbm, wq_hbm, wkv_hbm, wout_hbm, kv_hbm, out_ref,
     hidden, wq, wkv, wout, held0, held1, held2, held3, slots_in, slots_smem,
     ysend, yrecv, squares, q_acc, kv_acc, qown, qall, piece, pieces, turn,
-    acc, stat_m, stat_l, vt, turn_o, turn_lse,
-    part_out, part_in, lse_out, lse_in, att_out, att_all, sum_out, sum_in,
+    acc, stat_m, stat_l, vt, turn_o, turn_m, turn_l,
+    part_out_a, part_in_a, stat_out_a, stat_in_a, part_out_b, part_in_b, stat_out_b, stat_in_b,
+    att_out_a, att_out_b, att_a, att_b, sum_out_a, sum_in_a, sum_out_b, sum_in_b,
     load_sem, wout_load_sem, slot_sem, zk_s, zk_r, zs_s, zs_r, zp_s, zp_r, y_s, y_r,
     xq_s, xq_r, xt_s, xt_r, xw_s, xw_r, xo_s, xo_r, xl_s, xl_r, xa_s, xa_r, zo_s, zo_r,
 ):
@@ -151,17 +155,27 @@
         kv_acc[...] += lax.dot_general(normed, wkv[:, cols], NT, preferred_element_type=F32)
 
     queries = q_acc[...].astype(BF16)
-    qown[:ROWS, :] = queries[:, :HD]
-    qown[ROWS:, :] = queries[:, HD:]
-    own_rows = pl.ds(pl.multiple_of(x * 2 * ROWS, 16), 2 * ROWS)
-
-    def q_copy(d):
-        return remote(qown, qall.at[own_rows], xq_s.at[d], xq_r.at[d], x_peer(d))
-
-    for d in FAR_FIRST:
-        q_copy(d).start()
-    qall[own_rows, :] = qown[...]
-    qall[pl.ds(QROWS, QPAD - QROWS), :] = jnp.zeros((QPAD - QROWS, HD), BF16)
+    for h in range(2):
+        head = queries[:, h * HD:(h + 1) * HD]
+        qown[h * SPAN:(h + 1) * SPAN, :] = head[:SPAN]
+        qown[PAIR + h * SPAN:PAIR + (h + 1) * SPAN, :] = head[SPAN:2 * SPAN]
+        qown[2 * PAIR + h * SAMP:2 * PAIR + (h + 1) * SAMP, :] = head[2 * SPAN:]
+
+    rows_a = pl.ds(pl.multiple_of(x * PAIR, PAIR), PAIR)
+    rows_b = pl.ds(pl.multiple_of(GROUP * SPAN + x * PAIR, PAIR), PAIR)
+    rows_c = pl.ds(2 * GROUP * SPAN, GROUP * SAMP)
+    own_rows = (rows_a, rows_b, pl.ds(pl.multiple_of(2 * GROUP * SPAN + x * 2 * SAMP, 2 * SAMP), 2 * SAMP))
+    made_rows = (pl.ds(0, PAIR), pl.ds(PAIR, PAIR), pl.ds(2 * PAIR, 2 * SAMP))
+
+    def q_copy(d, n):
+        return remote(
+            qown.at[made_rows[n]], qall.at[own_rows[n]], xq_s.at[d * 3 + n], xq_r.at[d * 3 + n], x_peer(d))
+
+    for n in range(3):
+        for d in FAR_FIRST:
+            q_copy(d, n).start()
+        qall[own_rows[n], :] = qown[made_rows[n], :]
+    qall[QROWS:, :] = jnp.zeros((QPAD - QROWS, HD), BF16)
 
     half = kv_acc[...]
     blank = jnp.zeros_like(half)
@@ -188,8 +202,6 @@
     acc[...] = jnp.zeros_like(acc)
     stat_m[...] = jnp.full_like(stat_m, -DEAD)
     stat_l[...] = jnp.zeros_like(stat_l)
-    for d in (1, 2, 3):
-        q_copy(d).wait()
 
     def turn_copy(d, kind):
         return remote(
@@ -202,6 +214,62 @@
         to_smem.start()
         to_smem.wait()
         pass_on(k, d)
+
+    arrived(1, 1)
+    arrived(3, 2)
+    page_copy(2).start()
+    for d in (1, 2, 3):
+        for n in range(3):
+            q_copy(d, n).wait()
+
+    def o_copy(d, part):
+        out, into = ((part_out_a, part_in_a), (part_out_b, part_in_b))[part]
+        return remote(out.at[d], into.at[d], xo_s.at[d * 2 + part], xo_r.at[d * 2 + part], x_peer(d))
+
+    def l_copy(d, part):
+        out, into = ((stat_out_a, stat_in_a), (stat_out_b, stat_in_b))[part]
+        return remote(out.at[d], into.at[d], xl_s.at[d * 2 + part], xl_r.at[d * 2 + part], x_peer(d))
+
+    def send_part(part):
+        for d in FAR_FIRST:
+            start = ((x + d) % 4) * PAIR
+            if part == 0:
+                cols = pl.ds(pl.multiple_of(start, PAIR), PAIR)
+                part_out_a[d] = acc[:, cols].astype(BF16)
+                stat_out_a[d, 0:1, :] = stat_m[:, cols]
+                stat_out_a[d, 1:2, :] = stat_l[:, cols]
+            else:
+                cols = pl.ds(pl.multiple_of(GROUP * SPAN + start, PAIR), PAIR)
+                part_out_b[d, :, :PAIR] = acc[:, cols].astype(BF16)
+                part_out_b[d, :, PAIR:] = acc[:, rows_c].astype(BF16)
+                stat_out_b[d, 0:1, :PAIR] = stat_m[:, cols]
+                stat_out_b[d, 0:1, PAIR:] = stat_m[:, rows_c]
+                stat_out_b[d, 1:2, :PAIR] = stat_l[:, cols]
+                stat_out_b[d, 1:2, PAIR:] = stat_l[:, rows_c]
+            l_copy(d, part).start()
+            o_copy(d, part).start()
+
+    def own_turn():
+        for d in (1, 2, 3):
+            for kind in range(2):
+                turn_copy(d, kind).wait()
+        pair = (z % 2) * 2
+        turn_keys = turn[0, pair] + turn[0, pair + 1]
+        turn_values = turn[1, pair] + turn[1, pair + 1]
+        rows = jnp.concatenate([qall[rows_a, :], qall[rows_b, :], qall[rows_c, :]], axis=0)
+        count = 2 * PAIR + GROUP * SAMP
+        scores = lax.dot_general(turn_keys, rows, NT, preferred_element_type=F32)
+        key_idx = lax.broadcasted_iota(jnp.int32, (ROWS, count), 0)
+        place = lax.broadcasted_iota(jnp.int32, (ROWS, count), 1)
+        token = jnp.where(
+            place < PAIR, place % SPAN, jnp.where(place < 2 * PAIR, SPAN + place % SPAN, 2 * SPAN + place % SAMP))
+        allowed = (key_idx <= token) & ((key_idx < ROWS - SAMP) | (key_idx == token))
+        scores = jnp.where(allowed, scores, -DEAD)
+        top = jnp.max(scores, axis=0, keepdims=True)
+        probs = jnp.exp2(scores * scale - top * scale)
+        turn_m[...] = top
+        turn_l[...] = jnp.sum(probs, axis=0, keepdims=True)
+        turn_o[...] = lax.dot_general(turn_values.T, probs.astype(BF16), NN, preferred_element_type=F32)
 
     def visit(n, carry):
         k, first = n // 2, (n % 2) * CHUNK
@@ -223,36 +291,42 @@
         keys = pages[:, :, :PAGE, :].reshape(KEYS, HD)
         vt[...] = pages[:, :, PAGE:, :].reshape(KEYS, HD).T
 
-        @pl.loop(0, TILES // UNROLL)
-        def _(t):
-            cols = [pl.ds(pl.multiple_of((t * UNROLL + u) * TILE, TILE), TILE) for u in range(UNROLL)]
-            all_scores = [
-                lax.dot_general(keys, qall[cols[u], :], NT, preferred_element_type=F32) for u in range(UNROLL)]
-            for u in range(UNROLL):
-                scores = all_scores[u]
-                old_m = stat_m[:, cols[u]]
+        def attend(tiles):
+            cols = [pl.ds(t * TILE, TILE) for t in tiles]
+            all_scores = [lax.dot_general(keys, qall[own, :], NT, preferred_element_type=F32) for own in cols]
+            for own, scores in zip(cols, all_scores):
+                old_m = stat_m[:, own]
                 new_m = old_m
                 for j in range(CHUNK * CAP):
                     top = jnp.max(scores[j * PAGE:(j + 1) * PAGE], axis=0, keepdims=True)
                     new_m = jnp.maximum(new_m, jnp.where(live[j], top, -DEAD))
                 shift = new_m * scale
                 shrink = jnp.exp2(old_m * scale - shift)
-                total = stat_l[:, cols[u]] * shrink
+                total = stat_l[:, own] * shrink
                 weights = []
                 for j in range(CHUNK * CAP):
                     probs = jnp.exp2(scores[j * PAGE:(j + 1) * PAGE] * scale - jnp.where(live[j], shift, DEAD))
                     total = total + jnp.sum(probs, axis=0, keepdims=True)
                     weights.append(probs.astype(BF16))
                 blended = lax.dot_general(vt[...], jnp.concatenate(weights, axis=0), NN, preferred_element_type=F32)
-                acc[:, cols[u]] = acc[:, cols[u]] * shrink + blended
-                stat_m[:, cols[u]] = new_m
-                stat_l[:, cols[u]] = total
+                acc[:, own] = acc[:, own] * shrink + blended
+                stat_m[:, own] = new_m
+                stat_l[:, own] = total
+
+        attend(FIRST_TILES)
+
+        @pl.when(n == STEPS - 1)
+        def _():
+            send_part(0)
+
+        attend(LATER_TILES)
+
+        @pl.when(n == STEPS - 1)
+        def _():
+            send_part(1)
 
         @pl.when(n == 0)
         def _():
-            arrived(1, 1)
-            arrived(3, 2)
-            page_copy(2).start()
             for d in (1, 2, 3):
                 piece_copy(d).wait()
             for d in FAR_FIRST:
@@ -270,88 +344,88 @@
         def _():
             arrived(2, 3)
 
+        @pl.when(n == 5)
+        def _():
+            own_turn()
+
         return carry
 
-    lax.fori_loop(0, 2 * 4, visit, 0)
-
-    for d in (1, 2, 3):
-        for kind in range(2):
-            turn_copy(d, kind).wait()
-    pair = (z % 2) * 2
-    turn_k = turn[0, pair] + turn[0, pair + 1]
-    turn_v = turn[1, pair] + turn[1, pair + 1]
-    block = pl.ds(pl.multiple_of(x * BLOCK, 128), BLOCK)
-    turn_scores = lax.dot_general(turn_k, qall[block, :], NT, preferred_element_type=F32)
-    key_idx = lax.broadcasted_iota(jnp.int32, (ROWS, BLOCK), 0)
-    row_idx = (lax.broadcasted_iota(jnp.int32, (ROWS, BLOCK), 1) + x * BLOCK) % ROWS
-    allowed = (key_idx <= row_idx) & ((key_idx < ROWS - SAMP) | (key_idx == row_idx))
-    turn_scores = jnp.where(allowed, turn_scores, -DEAD)
-    turn_m = jnp.max(turn_scores, axis=0, keepdims=True)
-    turn_p = jnp.exp2(turn_scores * scale - turn_m * scale)
-    turn_l = jnp.sum(turn_p, axis=0, keepdims=True)
-    turn_o[...] = lax.dot_general(turn_v.T, turn_p.astype(BF16), NN, preferred_element_type=F32) / turn_l
-    turn_lse[...] = turn_m * scale + jnp.log2(turn_l)
-
-    def o_copy(d):
-        return remote(part_out.at[d], part_in.at[d], xo_s.at[d], xo_r.at[d], x_peer(d))
-
-    def l_copy(d):
-        return remote(lse_out.at[d], lse_in.at[d], xl_s.at[d], xl_r.at[d], x_peer(d))
-
+    lax.fori_loop(0, STEPS, visit, 0)
+
+    def merge(own, part, turn_cols):
+        into, stats = ((part_in_a, stat_in_a), (part_in_b, stat_in_b))[part]
+        for d in (1, 2, 3):
+            l_copy(d, part).wait()
+            o_copy(d, part).wait()
+        tops = [jnp.concatenate([stat_m[:, cols] for cols in own], axis=1) * scale, turn_m[:, turn_cols] * scale]
+        sums = [jnp.concatenate([stat_l[:, cols] for cols in own], axis=1), turn_l[:, turn_cols]]
+        sources = [jnp.concatenate([acc[:, cols] for cols in own], axis=1), turn_o[:, turn_cols]]
+        for d in (1, 2, 3):
+            tops.append(stats[d, 0:1, :] * scale)
+            sums.append(stats[d, 1:2, :])
+            sources.append(into[d].astype(F32))
+        top = tops[0]
+        for other in tops[1:]:
+            top = jnp.maximum(top, other)
+        shares = [jnp.exp2(one - top) for one in tops]
+        norm = sums[0] * shares[0]
+        for one, share in zip(sums[1:], shares[1:]):
+            norm = norm + one * share
+        inverse = 1.0 / norm
+        merged = sources[0] * (shares[0] * inverse)
+        for one, share in zip(sources[1:], shares[1:]):
+            merged = merged + one * (share * inverse)
+        return merged
+
+    def a_copy(d, part):
+        out, into = ((att_out_a, att_a), (att_out_b, att_b))[part]
+        return remote(out, into.at[rows_a], xa_s.at[d * 2 + part], xa_r.at[d * 2 + part], x_peer(d))
+
+    att_out_a[...] = merge([rows_a], 0, pl.ds(0, PAIR)).T.astype(BF16)
     for d in FAR_FIRST:
-        cols = pl.ds(pl.multiple_of(((x + d) % 4) * BLOCK, 128), BLOCK)
-        total = jnp.maximum(stat_l[:, cols], 1e-30)
-        part_out[d] = (acc[:, cols] / total).astype(BF16)
-        lse_out[d] = jnp.broadcast_to(stat_m[:, cols] * scale + jnp.log2(total), (8, BLOCK))
-        o_copy(d).start()
-        l_copy(d).start()
-
-    own_l = jnp.maximum(stat_l[:, block], 1e-30)
-    own_lse = stat_m[:, block] * scale + jnp.log2(own_l)
-    for d in (1, 2, 3):
-        o_copy(d).wait()
-        l_copy(d).wait()
-    lses = [lse_in[d][:1] for d in (1, 2, 3)]
-    top = jnp.maximum(own_lse, turn_lse[...])
-    for lse in lses:
-        top = jnp.maximum(top, lse)
-    own_w = jnp.exp2(own_lse - top)
-    turn_w = jnp.exp2(turn_lse[...] - top)
-    norm = own_w + turn_w
-    merged = acc[:, block] * (own_w / own_l) + turn_o[...] * turn_w
-    for d in (1, 2, 3):
-        w = jnp.exp2(lses[d - 1] - top)
-        norm = norm + w
-        merged = merged + part_in[d].astype(F32) * w
-    att_out[...] = (merged / norm).T.astype(BF16)
-
-    def a_copy(d):
-        return remote(att_out, att_all.at[block], xa_s.at[d], xa_r.at[d], x_peer(d))
-
+        a_copy(d, 0).start()
+    att_a[rows_a, :] = att_out_a[...]
+    merged = merge([rows_b, rows_c], 1, pl.ds(PAIR, PAIR + GROUP * SAMP)).T.astype(BF16)
+    att_out_b[...] = merged[:PAIR]
     for d in FAR_FIRST:
-        a_copy(d).start()
-    att_all[block, :] = att_out[...]
+        a_copy(d, 1).start()
+    att_b[rows_a, :] = att_out_b[...]
+    samples = jnp.concatenate(
+        [merged[PAIR + h * SAMP:PAIR + (h + 1) * SAMP] for h in range(GROUP)], axis=1)
+
+    def z_copy(d, part):
+        out, into = ((sum_out_a, sum_in_a), (sum_out_b, sum_in_b))[part]
+        return remote(out.at[d], into.at[d], zo_s.at[d * 2 + part], zo_r.at[d * 2 + part], z_peer(d))
+
     for d in (1, 2, 3):
         for m in range(4):
             wout_copy(d, m).wait()
     for m in range(4):
         own_wout(m).wait()
-    for d in (1, 2, 3):
-        a_copy(d).wait()
-
-    attended = jnp.concatenate([att_all[h * ROWS:(h + 1) * ROWS, :] for h in range(GROUP)], axis=1)
-
-    def z_copy(d):
-        return remote(sum_out.at[d], sum_in.at[d], zo_s.at[d], zo_r.at[d], z_peer(d))
-
+
+    for d in (1, 2, 3):
+        a_copy(d, 0).wait()
+    early = jnp.concatenate([att_a[h * SPAN:(h + 1) * SPAN, :] for h in range(GROUP)], axis=1)
     for d in FAR_FIRST:
-        sum_out[d] = jnp.dot(attended, wout[(z + d) % 4], preferred_element_type=F32).astype(BF16)
-        z_copy(d).start()
-    result = jnp.dot(attended, wout[z], preferred_element_type=F32)
-    for d in (1, 2, 3):
-        z_copy(d).wait()
-        result = result + sum_in[d].astype(F32)
-    out_ref[...] = result.astype(BF16)
+        sum_out_a[d] = jnp.dot(early, wout[(z + d) % 4], preferred_element_type=F32).astype(BF16)
+        z_copy(d, 0).start()
+    for d in (1, 2, 3):
+        a_copy(d, 1).wait()
+    late = jnp.concatenate([att_b[h * SPAN:(h + 1) * SPAN, :] for h in range(GROUP)], axis=1)
+    late = jnp.concatenate([late, samples], axis=0)
+    for d in FAR_FIRST:
+        sum_out_b[d] = jnp.dot(late, wout[(z + d) % 4], preferred_element_type=F32).astype(BF16)
+        z_copy(d, 1).start()
+    early_out = jnp.dot(early, wout[z], preferred_element_type=F32)
+    late_out = jnp.dot(late, wout[z], preferred_element_type=F32)
+    for d in (1, 2, 3):
+        z_copy(d, 0).wait()
+        early_out = early_out + sum_in_a[d].astype(F32)
+    out_ref[:SPAN, :] = early_out.astype(BF16)
+    for d in (1, 2, 3):
+        z_copy(d, 1).wait()
+        late_out = late_out + sum_in_b[d].astype(F32)
+    out_ref[SPAN:, :] = late_out.astype(BF16)
 
     for d in (1, 2, 3):
         page_copy(d).wait_send()
@@ -400,22 +474,31 @@
             pltpu.VMEM((1, QPAD), F32),
             pltpu.VMEM((1, QPAD), F32),
             pltpu.VMEM((HD, KEYS), BF16),
-            pltpu.VMEM((HD, BLOCK), F32),
-            pltpu.VMEM((1, BLOCK), F32),
-            pltpu.VMEM((4, HD, BLOCK), BF16),
-            pltpu.VMEM((4, HD, BLOCK), BF16),
-            pltpu.VMEM((4, 8, BLOCK), F32),
-            pltpu.VMEM((4, 8, BLOCK), F32),
-            pltpu.VMEM((BLOCK, HD), BF16),
-            pltpu.VMEM((QPAD, HD), BF16),
-            pltpu.VMEM((4, ROWS, OUT), BF16),
-            pltpu.VMEM((4, ROWS, OUT), BF16),
+            pltpu.VMEM((HD, 2 * PAIR + 128), F32),
+            pltpu.VMEM((1, 2 * PAIR + 128), F32),
+            pltpu.VMEM((1, 2 * PAIR + 128), F32),
+            pltpu.VMEM((4, HD, PAIR), BF16),
+            pltpu.VMEM((4, HD, PAIR), BF16),
+            pltpu.VMEM((4, 8, PAIR), F32),
+            pltpu.VMEM((4, 8, PAIR), F32),
+            pltpu.VMEM((4, HD, PAIR + 128), BF16),
+            pltpu.VMEM((4, HD, PAIR + 128), BF16),
+            pltpu.VMEM((4, 8, PAIR + 128), F32),
+            pltpu.VMEM((4, 8, PAIR + 128), F32),
+            pltpu.VMEM((PAIR, HD), BF16),
+            pltpu.VMEM((PAIR, HD), BF16),
+            pltpu.VMEM((4 * PAIR, HD), BF16),
+            pltpu.VMEM((4 * PAIR, HD), BF16),
+            pltpu.VMEM((4, SPAN, OUT), BF16),
+            pltpu.VMEM((4, SPAN, OUT), BF16),
+            pltpu.VMEM((4, LATE, OUT), BF16),
+            pltpu.VMEM((4, LATE, OUT), BF16),
             dma((4,)), dma((4,)), dma((4,)),
             dma((4,)), dma((4,)), dma((4,)), dma((4,)), dma((4,)), dma((4,)),
             dma((4 * SOURCES,)), dma((4 * SOURCES,)),
-            dma((4,)), dma((4,)), dma((8,)), dma((8,)), dma((16,)), dma((16,)),
-            dma((4,)), dma((4,)), dma((4,)), dma((4,)), dma((4,)), dma((4,)),
-            dma((4,)), dma((4,)),
+            dma((12,)), dma((12,)), dma((8,)), dma((8,)), dma((16,)), dma((16,)),
+            dma((8,)), dma((8,)), dma((8,)), dma((8,)), dma((8,)), dma((8,)),
+            dma((8,)), dma((8,)),
         ],
         compiler_params=pltpu.CompilerParams(
             collective_id=1, has_side_effects=True, vmem_limit_bytes=62 * 2**20),

time: 131 us -> 123 us (0.939)
  Pallas kernels: 128 us -> 119 us
    pallas_call x1, Pallas kernels: 128 us -> 119 us  [local(): pl.pallas_call(layer_kernel, out_shape=jax.ShapeDtypeStruct((ROWS, OUT),...]
where the time goes in v3:
time: 123 us
  Pallas kernels  119 us (97%)
  local copies, waits for them, and re-layouts  3.04 us (2%)
    pallas_call x1, Pallas kernels, local(): pl.pallas_call(layer_kernel, out_shape=jax.ShapeDtypeStruct((ROWS, OUT),...  119 us

profile of v3, /device:TPU:1, one launch (start us, length us, event | category | flops | bytes accessed | tf_op | source)
XLA Modules:
  0.0 122.5 jit_solution(10788013043444802920)
XLA Ops:
  0.0 0.8 copy.10
  0.8 0.6 pad.4.slots_ref
  1.4 119.5 %layer.1 = bf16[272,512]{1,0:T(8,128)(2,1)} custom-call(s32[8,128]{1,0:T(8,128)} %pad.4.slots_ref, s32[128]{0:T(128)} %bitcast.9, f32[1,8192]{1,0:T(1,128)} %bitcast.8, bf16[272,8192]{1,0:T(8,128)(2,1)} %hidden_hbm.1, bf16[8192,256]{1,0:T(8,128)(2,1)} %wq_hbm.1, bf16[64,8192]{1,0:T(8,128)(2,1)} %bitcast.7, bf16[256,8192]{1,0:T(8,128)(2,1)} %wout_hbm.1, ...), custom_call_target="tpu_custom_call" | custom-call | flops 16999999488 | bytes 19000000 | tf_op jit(solution)/shard_map/layer/pallas_call | solution.py:447
  120.8 1.7 %copy.12 = bf16[272,512]{1,0:T(8,128)(2,1)} copy(bf16[272,512]{1,0:T(8,128)(2,1)} %layer.1) | data formatting | bytes 557056

commit v4 on v3

--- a/solution.py
+++ b/solution.py
@@ -28,9 +28,11 @@
 FIRST_TILES = (0, 1, 2, 3)
 LATER_TILES = (4, 5, 6, 7, 8)
 SOURCES = 8
-CHUNK = 4
-STEPS = 8
-KEYS = CHUNK * CAP * PAGE
+EARLY_CHUNK = 4
+LAST_CHUNK = 2
+EARLY_STEPS = 3 * SOURCES // EARLY_CHUNK
+LAST_STEPS = SOURCES // LAST_CHUNK
+HALF = 256
 PART = 512
 OUT = 512
 NT = (((1,), (1,)), ((), ()))
@@ -50,20 +52,22 @@
 
 def layer_kernel(
     slots_ref, counts_ref, gain_ref, hidden_hbm, wq_hbm, wkv_hbm, wout_hbm, kv_hbm, out_ref,
-    hidden, wq, wkv, wout, held0, held1, held2, held3, slots_in, slots_smem,
+    hidden, wq, wkv, wout_x, wout_z, held0, keys1, values1, held2, held3, slots_out, slots_in, slots_smem,
     ysend, yrecv, squares, q_acc, kv_acc, qown, qall, piece, pieces, turn,
     acc, stat_m, stat_l, vt, turn_o, turn_m, turn_l,
     part_out_a, part_in_a, stat_out_a, stat_in_a, part_out_b, part_in_b, stat_out_b, stat_in_b,
-    att_out_a, att_out_b, att_a, att_b, sum_out_a, sum_in_a, sum_out_b, sum_in_b,
+    att_out_a, att_out_b, samples, att_xa, att_xb, att_za, att_zb,
+    sum_out_xa, sum_in_xa, sum_out_xb, sum_in_xb, sum_out_za, sum_in_za, sum_out_zb, sum_in_zb,
     load_sem, wout_load_sem, slot_sem, zk_s, zk_r, zs_s, zs_r, zp_s, zp_r, y_s, y_r,
-    xq_s, xq_r, xt_s, xt_r, xw_s, xw_r, xo_s, xo_r, xl_s, xl_r, xa_s, xa_r, zo_s, zo_r,
+    xq_s, xq_r, xt_s, xt_r, xw_s, xw_r, zw_s, zw_r,
+    xo_s, xo_r, xl_s, xl_r, xa_s, xa_r, za_s, za_r, xo2_s, xo2_r, zo_s, zo_r,
 ):
     pool = lax.axis_index("pool")
     tp = lax.axis_index("tp")
     y, c = pool // 2, pool % 2
     z, x = tp // 4, tp % 4
     scale = LOG2E / math.sqrt(HD)
-    held = (held0, held1, held2, held3)
+    held = (held0, None, held2, held3)
 
     def x_peer(d):
         return (pool, z * 4 + (x + d) % 4)
@@ -95,36 +99,60 @@
     ]
     for load in loads:
         load.start()
-    own_slots = pltpu.make_async_copy(slots_ref, slots_smem.at[0], slot_sem.at[0])
+    slots_out[:, :CAP] = slots_ref[...]
+    own_slots = pltpu.make_async_copy(slots_out, slots_smem.at[0], slot_sem.at[0])
     own_slots.start()
     pl.semaphore_wait(barrier, SOURCES - 1 + 6)
 
     def slot_copy(d):
-        return remote(slots_ref, slots_in.at[d], zs_s.at[d], zs_r.at[d], z_peer(d))
+        return remote(slots_out, slots_in.at[d], zs_s.at[d], zs_r.at[d], z_peer(d))
 
     def page_copy(d):
         return remote(kv_hbm.at[:, (z + d) % 4], held[d], zk_s.at[d], zk_r.at[d], z_peer(d))
 
+    def half_copy(half):
+        into = (keys1, values1)[half]
+        source = kv_hbm.at[:, (z + 1) % 4, pl.ds(half * PAGE, PAGE)]
+        return remote(source, into, zk_s.at[half], zk_r.at[half], z_peer(1))
+
     for d in (1, 3, 2):
         slot_copy(d).start()
-    for d in (1, 3):
-        page_copy(d).start()
+    half_copy(0).start()
+    page_copy(3).start()
 
     def y_copy(k, i):
         return remote(
             ysend.at[k, i], yrecv.at[k, i], y_s.at[k * SOURCES + i], y_r.at[k * SOURCES + i], (plane_peer(i), tp))
 
+    def half_y_copy(half, i):
+        rows = pl.ds(half * PAGE, PAGE)
+        own = (1 + 3 * half) * SOURCES + i
+        return remote(
+            ysend.at[1, i, :, rows], yrecv.at[1, i, :, rows], y_s.at[own], y_r.at[own], (plane_peer(i), tp))
+
     def pass_on(k, d):
         for slot in range(CAP):
             yrecv[k, 0, slot] = held[d][slots_smem[d, pool, slot]]
 
         @pl.loop(1, SOURCES)
-        def _(n):
-            i = jnp.where(n < SOURCES - 1, n + 1, 1)
+        def _(i):
             dest = plane_peer(i)
             for slot in range(CAP):
                 ysend[k, i, slot] = held[d][slots_smem[d, dest, slot]]
             y_copy(k, i).start()
+
+    def pass_half(half):
+        pages = (keys1, values1)[half]
+        rows = pl.ds(half * PAGE, PAGE)
+        for slot in range(CAP):
+            yrecv[1, 0, slot, rows] = pages[slots_smem[1, pool, slot]]
+
+        @pl.loop(1, SOURCES)
+        def _(i):
+            dest = plane_peer(i)
+            for slot in range(CAP):
+                ysend[1, i, slot, rows] = pages[slots_smem[1, dest, slot]]
+            half_y_copy(half, i).start()
 
     own_slots.wait()
     own_pages.wait()
@@ -141,6 +169,7 @@
         for m in range(PART // 128):
             squares[...] += part[:, m * 128:(m + 1) * 128]
 
+    half_copy(1).start()
     mean = jnp.sum(squares[...], axis=1, keepdims=True) * (1.0 / D)
     squares[...] = jnp.broadcast_to(lax.rsqrt(mean + 1e-05), squares.shape)
     q_acc[...] = jnp.zeros_like(q_acc)
@@ -189,15 +218,41 @@
         piece_copy(d).start()
     pieces[z] = piece[...]
 
-    def wout_copy(d, n):
-        columns = pl.ds(pl.multiple_of((n * 4 + (x + d) % 4) * OUT, OUT), OUT)
-        rows = pl.ds(pl.multiple_of(x * 256, 256), 256)
-        return remote(wout_hbm.at[:, columns], wout.at[n, rows], xw_s.at[d * 4 + n], xw_r.at[d * 4 + n], x_peer(d))
-
-    def own_wout(n):
-        columns = pl.ds(pl.multiple_of((n * 4 + x) * OUT, OUT), OUT)
-        rows = pl.ds(pl.multiple_of(x * 256, 256), 256)
-        return pltpu.make_async_copy(wout_hbm.at[:, columns], wout.at[n, rows], wout_load_sem.at[n])
+    def wout_columns(to_z, to_x, half):
+        return pl.ds(pl.multiple_of((to_z * 4 + to_x) * OUT + half * HALF, HALF), HALF)
+
+    def line_rows(place):
+        return pl.ds(pl.multiple_of(place * 256, 256), 256)
+
+    def wout_x_copy(d, n):
+        part = 2 * c + n
+        return remote(
+            wout_hbm.at[:, wout_columns(part, (x + d) % 4, 0)], wout_x.at[part, line_rows(x)],
+            xw_s.at[d * 2 + n], xw_r.at[d * 2 + n], x_peer(d))
+
+    def wout_z_copy(d, n):
+        part = 2 * c + n
+        return remote(
+            wout_hbm.at[:, wout_columns((z + d) % 4, part, 1)], wout_z.at[part, line_rows(z)],
+            zw_s.at[d * 2 + n], zw_r.at[d * 2 + n], z_peer(d))
+
+    def own_wout_x(n):
+        part = 2 * c + n
+        return pltpu.make_async_copy(
+            wout_hbm.at[:, wout_columns(part, x, 0)], wout_x.at[part, line_rows(x)], wout_load_sem.at[n])
+
+    def own_wout_z(n):
+        part = 2 * c + n
+        return pltpu.make_async_copy(
+            wout_hbm.at[:, wout_columns(z, part, 1)], wout_z.at[part, line_rows(z)], wout_load_sem.at[2 + n])
+
+    def wout_x_share(n):
+        part = 2 * c + n
+        return remote(wout_x.at[part], wout_x.at[part], xw_s.at[n], xw_r.at[n], (y * 2 + 1 - c, tp))
+
+    def wout_z_share(n):
+        part = 2 * c + n
+        return remote(wout_z.at[part], wout_z.at[part], zw_s.at[n], zw_r.at[n], (y * 2 + 1 - c, tp))
 
     acc[...] = jnp.zeros_like(acc)
     stat_m[...] = jnp.full_like(stat_m, -DEAD)
@@ -207,17 +262,17 @@
         return remote(
             pieces.at[kind * 2 + z // 2], turn.at[kind, x], xt_s.at[d * 2 + kind], xt_r.at[d * 2 + kind], x_peer(d))
 
-    def arrived(d, k):
-        page_copy(d).wait_recv()
+    def numbers_arrived(d):
         slot_copy(d).wait_recv()
         to_smem = pltpu.make_async_copy(slots_in.at[d], slots_smem.at[d], slot_sem.at[d])
         to_smem.start()
         to_smem.wait()
+
+    def arrived(d, k):
+        page_copy(d).wait_recv()
+        numbers_arrived(d)
         pass_on(k, d)
 
-    arrived(1, 1)
-    arrived(3, 2)
-    page_copy(2).start()
     for d in (1, 2, 3):
         for n in range(3):
             q_copy(d, n).wait()
@@ -271,62 +326,75 @@
         turn_l[...] = jnp.sum(probs, axis=0, keepdims=True)
         turn_o[...] = lax.dot_general(turn_values.T, probs.astype(BF16), NN, preferred_element_type=F32)
 
-    def visit(n, carry):
-        k, first = n // 2, (n % 2) * CHUNK
-
-        @pl.loop(0, CHUNK)
+    def attend(k, first, chunk, between=None):
+        slots = chunk * CAP
+
+        @pl.loop(0, chunk)
         def _(j):
-            @pl.when(first + j > 0)
+            @pl.when((first + j > 0) & (k != 1))
             def _():
                 y_copy(k, first + j).wait_recv()
 
+            @pl.when((first + j > 0) & (k == 1))
+            def _():
+                half_y_copy(0, first + j).wait_recv()
+                half_y_copy(1, first + j).wait_recv()
+
         live = []
-        for j in range(CHUNK):
+        for j in range(chunk):
             dy, dc = plane_offset(first + j)
             holder = (((y + 4 - dy) % 4) * 2 + (c + dc) % 2) * 16 + ((z + 4 - stage_offset(k)) % 4) * 4 + x
             count = counts_ref[holder]
             for slot in range(CAP):
                 live.append(count > slot)
-        pages = yrecv[k, pl.ds(first, CHUNK)]
-        keys = pages[:, :, :PAGE, :].reshape(KEYS, HD)
-        vt[...] = pages[:, :, PAGE:, :].reshape(KEYS, HD).T
-
-        def attend(tiles):
+        pages = yrecv[k, pl.ds(first, chunk)]
+        keys = pages[:, :, :PAGE, :].reshape(slots * PAGE, HD)
+        width = pl.ds(0, slots * PAGE)
+        vt[:, width] = pages[:, :, PAGE:, :].reshape(slots * PAGE, HD).T
+
+        def some(tiles):
             cols = [pl.ds(t * TILE, TILE) for t in tiles]
             all_scores = [lax.dot_general(keys, qall[own, :], NT, preferred_element_type=F32) for own in cols]
             for own, scores in zip(cols, all_scores):
                 old_m = stat_m[:, own]
                 new_m = old_m
-                for j in range(CHUNK * CAP):
+                for j in range(slots):
                     top = jnp.max(scores[j * PAGE:(j + 1) * PAGE], axis=0, keepdims=True)
                     new_m = jnp.maximum(new_m, jnp.where(live[j], top, -DEAD))
                 shift = new_m * scale
                 shrink = jnp.exp2(old_m * scale - shift)
                 total = stat_l[:, own] * shrink
                 weights = []
-                for j in range(CHUNK * CAP):
+                for j in range(slots):
                     probs = jnp.exp2(scores[j * PAGE:(j + 1) * PAGE] * scale - jnp.where(live[j], shift, DEAD))
                     total = total + jnp.sum(probs, axis=0, keepdims=True)
                     weights.append(probs.astype(BF16))
-                blended = lax.dot_general(vt[...], jnp.concatenate(weights, axis=0), NN, preferred_element_type=F32)
+                blended = lax.dot_general(
+                    vt[:, width], jnp.concatenate(weights, axis=0), NN, preferred_element_type=F32)
                 acc[:, own] = acc[:, own] * shrink + blended
                 stat_m[:, own] = new_m
                 stat_l[:, own] = total
 
-        attend(FIRST_TILES)
-
-        @pl.when(n == STEPS - 1)
-        def _():
-            send_part(0)
-
-        attend(LATER_TILES)
-
-        @pl.when(n == STEPS - 1)
-        def _():
-            send_part(1)
+        some(FIRST_TILES)
+        if between is not None:
+            between()
+        some(LATER_TILES)
+
+    def early_step(n, carry):
+        attend(n // 2, (n % 2) * EARLY_CHUNK, EARLY_CHUNK)
 
         @pl.when(n == 0)
         def _():
+            numbers_arrived(1)
+            half_copy(0).wait_recv()
+            pass_half(0)
+
+        @pl.when(n == 1)
+        def _():
+            half_copy(1).wait_recv()
+            pass_half(1)
+            arrived(3, 2)
+            page_copy(2).start()
             for d in (1, 2, 3):
                 piece_copy(d).wait()
             for d in FAR_FIRST:
@@ -335,22 +403,54 @@
             for kind in range(2):
                 turn[kind, x] = pieces[kind * 2 + z // 2]
             for d in FAR_FIRST:
-                for m in range(4):
-                    wout_copy(d, m).start()
-            for m in range(4):
-                own_wout(m).start()
+                for m in range(2):
+                    wout_x_copy(d, m).start()
+            for m in range(2):
+                own_wout_x(m).start()
+                own_wout_z(m).start()
+
+        @pl.when(n == 2)
+        def _():
+            own_turn()
 
         @pl.when(n == 3)
         def _():
             arrived(2, 3)
-
-        @pl.when(n == 5)
+            for d in FAR_FIRST:
+                for m in range(2):
+                    wout_z_copy(d, m).start()
+
+        return carry
+
+    def last_step(n, carry):
+        def when_last(part):
+            @pl.when(n == LAST_STEPS - 1)
+            def _():
+                send_part(part)
+
+        attend(3, n * LAST_CHUNK, LAST_CHUNK, lambda: when_last(0))
+        when_last(1)
+
+        @pl.when(n == 0)
         def _():
-            own_turn()
+            for m in range(2):
+                for d in (1, 2, 3):
+                    wout_x_copy(d, m).wait()
+                own_wout_x(m).wait()
+                wout_x_share(m).start()
+
+        @pl.when(n == 1)
+        def _():
+            for m in range(2):
+                for d in (1, 2, 3):
+                    wout_z_copy(d, m).wait()
+                own_wout_z(m).wait()
+                wout_z_share(m).start()
 
         return carry
 
-    lax.fori_loop(0, STEPS, visit, 0)
+    lax.fori_loop(0, EARLY_STEPS, early_step, 0)
+    lax.fori_loop(0, LAST_STEPS, last_step, 0)
 
     def merge(own, part, turn_cols):
         into, stats = ((part_in_a, stat_in_a), (part_in_b, stat_in_b))[part]
@@ -377,65 +477,103 @@
             merged = merged + one * (share * inverse)
         return merged
 
-    def a_copy(d, part):
-        out, into = ((att_out_a, att_a), (att_out_b, att_b))[part]
-        return remote(out, into.at[rows_a], xa_s.at[d * 2 + part], xa_r.at[d * 2 + part], x_peer(d))
+    def ax_copy(d, part):
+        out, into = ((att_out_a, att_xa), (att_out_b, att_xb))[part]
+        return remote(
+            out.at[pl.ds(0, PAIR)], into.at[rows_a], xa_s.at[d * 2 + part], xa_r.at[d * 2 + part], x_peer(d))
+
+    def az_copy(d, part):
+        out, into = ((att_out_a, att_za), (att_out_b, att_zb))[part]
+        return remote(out, into.at[z], za_s.at[d * 2 + part], za_r.at[d * 2 + part], z_peer(d))
 
     att_out_a[...] = merge([rows_a], 0, pl.ds(0, PAIR)).T.astype(BF16)
     for d in FAR_FIRST:
-        a_copy(d, 0).start()
-    att_a[rows_a, :] = att_out_a[...]
+        ax_copy(d, 0).start()
+        az_copy(d, 0).start()
+    att_xa[rows_a, :] = att_out_a[...]
+    att_za[z] = att_out_a[...]
     merged = merge([rows_b, rows_c], 1, pl.ds(PAIR, PAIR + GROUP * SAMP)).T.astype(BF16)
-    att_out_b[...] = merged[:PAIR]
+    samples[...] = merged[PAIR:]
+    att_out_b[:PAIR, :] = merged[:PAIR]
+    att_out_b[PAIR:, :] = samples[pl.ds(pl.multiple_of(x * 2 * SAMP, 2 * SAMP), 2 * SAMP), :]
     for d in FAR_FIRST:
-        a_copy(d, 1).start()
-    att_b[rows_a, :] = att_out_b[...]
-    samples = jnp.concatenate(
-        [merged[PAIR + h * SAMP:PAIR + (h + 1) * SAMP] for h in range(GROUP)], axis=1)
-
-    def z_copy(d, part):
-        out, into = ((sum_out_a, sum_in_a), (sum_out_b, sum_in_b))[part]
+        ax_copy(d, 1).start()
+        az_copy(d, 1).start()
+    att_xb[rows_a, :] = att_out_b[:PAIR, :]
+    att_zb[z] = att_out_b[...]
+
+    def sum_z_copy(d, part):
+        out, into = ((sum_out_za, sum_in_za), (sum_out_zb, sum_in_zb))[part]
         return remote(out.at[d], into.at[d], zo_s.at[d * 2 + part], zo_r.at[d * 2 + part], z_peer(d))
 
+    def sum_x_copy(d, part):
+        out, into = ((sum_out_xa, sum_in_xa), (sum_out_xb, sum_in_xb))[part]
+        return remote(out.at[d], into.at[d], xo2_s.at[d * 2 + part], xo2_r.at[d * 2 + part], x_peer(d))
+
+    def project(part, attended_x, attended_z):
+        out_x, out_z = ((sum_out_xa, sum_out_za), (sum_out_xb, sum_out_zb))[part]
+        for d in FAR_FIRST:
+            out_z[d] = jnp.dot(attended_x, wout_x[(z + d) % 4], preferred_element_type=F32).astype(BF16)
+            sum_z_copy(d, part).start()
+            out_x[d] = jnp.dot(attended_z, wout_z[(x + d) % 4], preferred_element_type=F32).astype(BF16)
+            sum_x_copy(d, part).start()
+
+    def line_up(ref, start, size):
+        return jnp.concatenate(
+            [ref[m, start + h * size:start + (h + 1) * size, :] for m in range(4) for h in range(2)], axis=1)
+
+    for m in range(2):
+        wout_x_share(m).wait()
+        wout_z_share(m).wait()
     for d in (1, 2, 3):
-        for m in range(4):
-            wout_copy(d, m).wait()
-    for m in range(4):
-        own_wout(m).wait()
-
+        ax_copy(d, 0).wait()
+        az_copy(d, 0).wait()
+    early_x = jnp.concatenate([att_xa[h * SPAN:(h + 1) * SPAN, :] for h in range(GROUP)], axis=1)
+    early_z = line_up(att_za, 0, SPAN)
+    project(0, early_x, early_z)
     for d in (1, 2, 3):
-        a_copy(d, 0).wait()
-    early = jnp.concatenate([att_a[h * SPAN:(h + 1) * SPAN, :] for h in range(GROUP)], axis=1)
-    for d in FAR_FIRST:
-        sum_out_a[d] = jnp.dot(early, wout[(z + d) % 4], preferred_element_type=F32).astype(BF16)
-        z_copy(d, 0).start()
+        ax_copy(d, 1).wait()
+        az_copy(d, 1).wait()
+    late_x = jnp.concatenate(
+        [
+            jnp.concatenate([att_xb[h * SPAN:(h + 1) * SPAN, :] for h in range(GROUP)], axis=1),
+            jnp.concatenate([samples[h * SAMP:(h + 1) * SAMP, :] for h in range(GROUP)], axis=1),
+        ],
+        axis=0)
+    late_z = jnp.concatenate([line_up(att_zb, 0, SPAN), line_up(att_zb, PAIR, SAMP)], axis=0)
+    project(1, late_x, late_z)
+    sums_z = [jnp.dot(one, wout_x[z], preferred_element_type=F32) for one in (early_x, late_x)]
+    sums_x = [jnp.dot(one, wout_z[x], preferred_element_type=F32) for one in (early_z, late_z)]
+    for part, rows in ((0, slice(0, SPAN)), (1, slice(SPAN, ROWS))):
+        sum_x, sum_z = sums_x[part], sums_z[part]
+        in_x, in_z = ((sum_in_xa, sum_in_za), (sum_in_xb, sum_in_zb))[part]
+        for d in (1, 2, 3):
+            sum_z_copy(d, part).wait()
+            sum_z = sum_z + in_z[d].astype(F32)
+            sum_x_copy(d, part).wait()
+            sum_x = sum_x + in_x[d].astype(F32)
+        out_ref[rows, :HALF] = sum_z.astype(BF16)
+        out_ref[rows, HALF:] = sum_x.astype(BF16)
+
     for d in (1, 2, 3):
-        a_copy(d, 1).wait()
-    late = jnp.concatenate([att_b[h * SPAN:(h + 1) * SPAN, :] for h in range(GROUP)], axis=1)
-    late = jnp.concatenate([late, samples], axis=0)
-    for d in FAR_FIRST:
-        sum_out_b[d] = jnp.dot(late, wout[(z + d) % 4], preferred_element_type=F32).astype(BF16)
-        z_copy(d, 1).start()
-    early_out = jnp.dot(early, wout[z], preferred_element_type=F32)
-    late_out = jnp.dot(late, wout[z], preferred_element_type=F32)
-    for d in (1, 2, 3):
-        z_copy(d, 0).wait()
-        early_out = early_out + sum_in_a[d].astype(F32)
-    out_ref[:SPAN, :] = early_out.astype(BF16)
-    for d in (1, 2, 3):
-        z_copy(d, 1).wait()
-        late_out = late_out + sum_in_b[d].astype(F32)
-    out_ref[SPAN:, :] = late_out.astype(BF16)
-
-    for d in (1, 2, 3):
+        slot_copy(d).wait_send()
+    for d in (2, 3):
         page_copy(d).wait_send()
-        slot_copy(d).wait_send()
+    for half in range(2):
+        half_copy(half).wait_send()
 
     @pl.loop(0, 4)
     def _(k):
         @pl.loop(1, SOURCES)
         def _(i):
-            y_copy(k, i).wait_send()
+            @pl.when(k != 1)
+            def _():
+                y_copy(k, i).wait_send()
+
+            @pl.when(k == 1)
+            def _():
+                half_y_copy(0, i).wait_send()
+                half_y_copy(1, i).wait_send()
 
 
 def local(hidden_in, norm_gain, w_query, w_keyval, w_out, kv_store, page_slots, page_counts):
@@ -443,7 +581,7 @@
     smem = pl.BlockSpec(memory_space=pltpu.SMEM)
     anywhere = pl.BlockSpec(memory_space=pl.ANY)
     dma = pltpu.SemaphoreType.DMA
-    slots = jnp.pad(page_slots[:, 0, :], ((0, 0), (0, 128 - CAP)))
+    slots = page_slots[:, 0, :]
     return pl.pallas_call(
         layer_kernel,
         out_shape=jax.ShapeDtypeStruct((ROWS, OUT), BF16),
@@ -453,11 +591,14 @@
             pltpu.VMEM((ROWS, D), BF16),
             pltpu.VMEM((D, 256), BF16),
             pltpu.VMEM((64, D), BF16),
-            pltpu.VMEM((4, 1024, OUT), BF16),
+            pltpu.VMEM((4, 1024, HALF), BF16),
+            pltpu.VMEM((4, 1024, HALF), BF16),
+            pltpu.VMEM((16, 2 * PAGE, HD), BF16),
+            pltpu.VMEM((16, PAGE, HD), BF16),
+            pltpu.VMEM((16, PAGE, HD), BF16),
             pltpu.VMEM((16, 2 * PAGE, HD), BF16),
             pltpu.VMEM((16, 2 * PAGE, HD), BF16),
-            pltpu.VMEM((16, 2 * PAGE, HD), BF16),
-            pltpu.VMEM((16, 2 * PAGE, HD), BF16),
+            pltpu.VMEM((8, 128), jnp.int32),
             pltpu.VMEM((4, 8, 128), jnp.int32),
             pltpu.SMEM((4, 8, 128), jnp.int32),
             pltpu.VMEM((4, SOURCES, CAP, 2 * PAGE, HD), BF16),
@@ -473,7 +614,7 @@
             pltpu.VMEM((HD, QPAD), F32),
             pltpu.VMEM((1, QPAD), F32),
             pltpu.VMEM((1, QPAD), F32),
-            pltpu.VMEM((HD, KEYS), BF16),
+            pltpu.VMEM((HD, EARLY_CHUNK * CAP * PAGE), BF16),
             pltpu.VMEM((HD, 2 * PAIR + 128), F32),
             pltpu.VMEM((1, 2 * PAIR + 128), F32),
             pltpu.VMEM((1, 2 * PAIR + 128), F32),
@@ -486,19 +627,27 @@
             pltpu.VMEM((4, 8, PAIR + 128), F32),
             pltpu.VMEM((4, 8, PAIR + 128), F32),
             pltpu.VMEM((PAIR, HD), BF16),
-            pltpu.VMEM((PAIR, HD), BF16),
+            pltpu.VMEM((PAIR + 2 * SAMP, HD), BF16),
+            pltpu.VMEM((GROUP * SAMP, HD), BF16),
             pltpu.VMEM((4 * PAIR, HD), BF16),
             pltpu.VMEM((4 * PAIR, HD), BF16),
-            pltpu.VMEM((4, SPAN, OUT), BF16),
-            pltpu.VMEM((4, SPAN, OUT), BF16),
-            pltpu.VMEM((4, LATE, OUT), BF16),
-            pltpu.VMEM((4, LATE, OUT), BF16),
+            pltpu.VMEM((4, PAIR, HD), BF16),
+            pltpu.VMEM((4, PAIR + 2 * SAMP, HD), BF16),
+            pltpu.VMEM((4, SPAN, HALF), BF16),
+            pltpu.VMEM((4, SPAN, HALF), BF16),
+            pltpu.VMEM((4, LATE, HALF), BF16),
+            pltpu.VMEM((4, LATE, HALF), BF16),
+            pltpu.VMEM((4, SPAN, HALF), BF16),
+            pltpu.VMEM((4, SPAN, HALF), BF16),
+            pltpu.VMEM((4, LATE, HALF), BF16),
+            pltpu.VMEM((4, LATE, HALF), BF16),
             dma((4,)), dma((4,)), dma((4,)),
             dma((4,)), dma((4,)), dma((4,)), dma((4,)), dma((4,)), dma((4,)),
-            dma((4 * SOURCES,)), dma((4 * SOURCES,)),
-            dma((12,)), dma((12,)), dma((8,)), dma((8,)), dma((16,)), dma((16,)),
+            dma((5 * SOURCES,)), dma((5 * SOURCES,)),
+            dma((12,)), dma((12,)), dma((8,)), dma((8,)), dma((8,)), dma((8,)),
+            dma((8,)), dma((8,)),
             dma((8,)), dma((8,)), dma((8,)), dma((8,)), dma((8,)), dma((8,)),
-            dma((8,)), dma((8,)),
+            dma((8,)), dma((8,)), dma((8,)), dma((8,)), dma((8,)), dma((8,)),
         ],
         compiler_params=pltpu.CompilerParams(
             collective_id=1, has_side_effects=True, vmem_limit_bytes=62 * 2**20),

time: 123 us -> 115 us (0.935)
  Pallas kernels: 119 us -> 111 us
    pallas_call x1, Pallas kernels: 119 us -> 111 us  [local(): pl.pallas_call(layer_kernel, out_shape=jax.ShapeDtypeStruct((ROWS, OUT),...]
where the time goes in v4:
time: 115 us; the launch traced here: 114 us
  Pallas kernels  111 us (97%)
  local copies, waits for them, and re-layouts  3.03 us (3%)
    pallas_call x1, Pallas kernels, local(): pl.pallas_call(layer_kernel, out_shape=jax.ShapeDtypeStruct((ROWS, OUT),...  111 us

profile of v4, /device:TPU:1, one launch (start us, length us, event | category | flops | bytes accessed | tf_op | source)
XLA Modules:
  0.0 114.4 jit_solution(6058155865604773313)
XLA Ops:
  0.0 1.3 %copy.10 = s32[8,1,3]{2,0,1:T(8,128)} copy(s32[8,1,3]{0,1,2:T(1,128)} %param.14) | data formatting | bytes 192 | tf_op jit(solution)/shard_map/squeeze | solution.py:584
  1.3 111.3 %layer.1 = bf16[272,512]{1,0:T(8,128)(2,1)} custom-call(s32[8,3]{1,0:T(8,128)} %bitcast.5, s32[128]{0:T(128)} %bitcast.9, f32[1,8192]{1,0:T(1,128)} %bitcast.8, bf16[272,8192]{1,0:T(8,128)(2,1)} %hidden_hbm.1, bf16[8192,256]{1,0:T(8,128)(2,1)} %wq_hbm.1, bf16[64,8192]{1,0:T(8,128)(2,1)} %bitcast.7, bf16[256,8192]{1,0:T(8,128)(2,1)} %wout_hbm.1, ...), custom_call_target="tpu_custom_call" | custom-call | flops 16999999488 | bytes 19000000 | tf_op jit(solution)/shard_map/layer/pallas_call | solution.py:585
  112.7 1.7 %copy.12 = bf16[272,512]{1,0:T(8,128)(2,1)} copy(bf16[272,512]{1,0:T(8,128)(2,1)} %layer.1) | data formatting | bytes 557056

commit v5 on v4

--- a/solution.py
+++ b/solution.py
@@ -21,12 +21,12 @@
 GROUP = 8
 SPAN = 128
 PAIR = 2 * SPAN
-LATE = 144
+EARLY = 144
 QROWS = GROUP * ROWS
 QPAD = 2304
 TILE = 256
-FIRST_TILES = (0, 1, 2, 3)
-LATER_TILES = (4, 5, 6, 7, 8)
+FIRST_TILES = (0, 1, 2, 3, 8)
+LATER_TILES = (4, 5, 6, 7)
 SOURCES = 8
 EARLY_CHUNK = 4
 LAST_CHUNK = 2
@@ -51,8 +51,8 @@
 
 
 def layer_kernel(
-    slots_ref, counts_ref, gain_ref, hidden_hbm, wq_hbm, wkv_hbm, wout_hbm, kv_hbm, out_ref,
-    hidden, wq, wkv, wout_x, wout_z, held0, keys1, values1, held2, held3, slots_out, slots_in, slots_smem,
+    slots_hbm, counts_hbm, gain_hbm, hidden_hbm, wq_hbm, wkv_hbm, wout_hbm, kv_hbm, out_ref,
+    counts_ref, gain_ref, slots_own, hidden, wq, wkv, wout_x, wout_z, held0, keys1, values1, held2, held3, slots_out, slots_in, slots_smem,
     ysend, yrecv, squares, q_acc, kv_acc, qown, qall, piece, pieces, turn,
     acc, stat_m, stat_l, vt, turn_o, turn_m, turn_l,
     part_out_a, part_in_a, stat_out_a, stat_in_a, part_out_b, part_in_b, stat_out_b, stat_in_b,
@@ -83,6 +83,17 @@
         return pltpu.make_async_remote_copy(
             src_ref=src, dst_ref=dst, send_sem=send_sem, recv_sem=recv_sem, device_id=device, device_id_type=MESH)
 
+    own_pages = pltpu.make_async_copy(kv_hbm.at[:, z], held0, load_sem.at[0])
+    own_pages.start()
+    fetch_slots = pltpu.make_async_copy(slots_hbm, slots_own, load_sem.at[4])
+    fetch_slots.start()
+    loads = [
+        pltpu.make_async_copy(hidden_hbm, hidden, load_sem.at[1]),
+        pltpu.make_async_copy(wq_hbm, wq, load_sem.at[2]),
+        pltpu.make_async_copy(wkv_hbm, wkv, load_sem.at[3]),
+        pltpu.make_async_copy(gain_hbm, gain_ref, load_sem.at[5]),
+        pltpu.make_async_copy(counts_hbm, counts_ref, load_sem.at[6]),
+    ]
     barrier = pltpu.get_barrier_semaphore()
     for i in range(1, SOURCES):
         pl.semaphore_signal(barrier, inc=1, device_id=(plane_peer(i), tp), device_id_type=MESH)
@@ -90,16 +101,11 @@
         pl.semaphore_signal(barrier, inc=1, device_id=x_peer(d), device_id_type=MESH)
         pl.semaphore_signal(barrier, inc=1, device_id=z_peer(d), device_id_type=MESH)
 
-    own_pages = pltpu.make_async_copy(kv_hbm.at[:, z], held0, load_sem.at[0])
-    own_pages.start()
-    loads = [
-        pltpu.make_async_copy(hidden_hbm, hidden, load_sem.at[1]),
-        pltpu.make_async_copy(wq_hbm, wq, load_sem.at[2]),
-        pltpu.make_async_copy(wkv_hbm, wkv, load_sem.at[3]),
-    ]
     for load in loads:
         load.start()
-    slots_out[:, :CAP] = slots_ref[...]
+    fetch_slots.wait()
+    for slot in range(CAP):
+        slots_out[slot:slot + 1, :8] = slots_own[slot]
     own_slots = pltpu.make_async_copy(slots_out, slots_smem.at[0], slot_sem.at[0])
     own_slots.start()
     pl.semaphore_wait(barrier, SOURCES - 1 + 6)
@@ -132,26 +138,26 @@
 
     def pass_on(k, d):
         for slot in range(CAP):
-            yrecv[k, 0, slot] = held[d][slots_smem[d, pool, slot]]
+            yrecv[k, 0, slot] = held[d][slots_smem[d, slot, pool]]
 
         @pl.loop(1, SOURCES)
         def _(i):
             dest = plane_peer(i)
             for slot in range(CAP):
-                ysend[k, i, slot] = held[d][slots_smem[d, dest, slot]]
+                ysend[k, i, slot] = held[d][slots_smem[d, slot, dest]]
             y_copy(k, i).start()
 
     def pass_half(half):
         pages = (keys1, values1)[half]
         rows = pl.ds(half * PAGE, PAGE)
         for slot in range(CAP):
-            yrecv[1, 0, slot, rows] = pages[slots_smem[1, pool, slot]]
+            yrecv[1, 0, slot, rows] = pages[slots_smem[1, slot, pool]]
 
         @pl.loop(1, SOURCES)
         def _(i):
             dest = plane_peer(i)
             for slot in range(CAP):
-                ysend[1, i, slot, rows] = pages[slots_smem[1, dest, slot]]
+                ysend[1, i, slot, rows] = pages[slots_smem[1, slot, dest]]
             half_y_copy(half, i).start()
 
     own_slots.wait()
@@ -290,17 +296,17 @@
             start = ((x + d) % 4) * PAIR
             if part == 0:
                 cols = pl.ds(pl.multiple_of(start, PAIR), PAIR)
-                part_out_a[d] = acc[:, cols].astype(BF16)
-                stat_out_a[d, 0:1, :] = stat_m[:, cols]
-                stat_out_a[d, 1:2, :] = stat_l[:, cols]
+                part_out_a[d, :, :PAIR] = acc[:, cols].astype(BF16)
+                part_out_a[d, :, PAIR:] = acc[:, rows_c].astype(BF16)
+                stat_out_a[d, 0:1, :PAIR] = stat_m[:, cols]
+                stat_out_a[d, 0:1, PAIR:] = stat_m[:, rows_c]
+                stat_out_a[d, 1:2, :PAIR] = stat_l[:, cols]
+                stat_out_a[d, 1:2, PAIR:] = stat_l[:, rows_c]
             else:
                 cols = pl.ds(pl.multiple_of(GROUP * SPAN + start, PAIR), PAIR)
-                part_out_b[d, :, :PAIR] = acc[:, cols].astype(BF16)
-                part_out_b[d, :, PAIR:] = acc[:, rows_c].astype(BF16)
-                stat_out_b[d, 0:1, :PAIR] = stat_m[:, cols]
-                stat_out_b[d, 0:1, PAIR:] = stat_m[:, rows_c]
-                stat_out_b[d, 1:2, :PAIR] = stat_l[:, cols]
-                stat_out_b[d, 1:2, PAIR:] = stat_l[:, rows_c]
+                part_out_b[d] = acc[:, cols].astype(BF16)
+                stat_out_b[d, 0:1, :] = stat_m[:, cols]
+                stat_out_b[d, 1:2, :] = stat_l[:, cols]
             l_copy(d, part).start()
             o_copy(d, part).start()
 
@@ -311,13 +317,14 @@
         pair = (z % 2) * 2
         turn_keys = turn[0, pair] + turn[0, pair + 1]
         turn_values = turn[1, pair] + turn[1, pair + 1]
-        rows = jnp.concatenate([qall[rows_a, :], qall[rows_b, :], qall[rows_c, :]], axis=0)
+        rows = jnp.concatenate([qall[rows_a, :], qall[rows_c, :], qall[rows_b, :]], axis=0)
         count = 2 * PAIR + GROUP * SAMP
         scores = lax.dot_general(turn_keys, rows, NT, preferred_element_type=F32)
         key_idx = lax.broadcasted_iota(jnp.int32, (ROWS, count), 0)
         place = lax.broadcasted_iota(jnp.int32, (ROWS, count), 1)
         token = jnp.where(
-            place < PAIR, place % SPAN, jnp.where(place < 2 * PAIR, SPAN + place % SPAN, 2 * SPAN + place % SAMP))
+            place < PAIR, place % SPAN,
+            jnp.where(place < PAIR + GROUP * SAMP, 2 * SPAN + place % SAMP, SPAN + place % SPAN))
         allowed = (key_idx <= token) & ((key_idx < ROWS - SAMP) | (key_idx == token))
         scores = jnp.where(allowed, scores, -DEAD)
         top = jnp.max(scores, axis=0, keepdims=True)
@@ -344,7 +351,7 @@
         for j in range(chunk):
             dy, dc = plane_offset(first + j)
             holder = (((y + 4 - dy) % 4) * 2 + (c + dc) % 2) * 16 + ((z + 4 - stage_offset(k)) % 4) * 4 + x
-            count = counts_ref[holder]
+            count = counts_ref[0, holder]
             for slot in range(CAP):
                 live.append(count > slot)
         pages = yrecv[k, pl.ds(first, chunk)]
@@ -486,20 +493,20 @@
         out, into = ((att_out_a, att_za), (att_out_b, att_zb))[part]
         return remote(out, into.at[z], za_s.at[d * 2 + part], za_r.at[d * 2 + part], z_peer(d))
 
-    att_out_a[...] = merge([rows_a], 0, pl.ds(0, PAIR)).T.astype(BF16)
+    merged = merge([rows_a, rows_c], 0, pl.ds(0, PAIR + GROUP * SAMP)).T.astype(BF16)
+    samples[...] = merged[PAIR:]
+    att_out_a[:PAIR, :] = merged[:PAIR]
+    att_out_a[PAIR:, :] = samples[pl.ds(pl.multiple_of(x * 2 * SAMP, 2 * SAMP), 2 * SAMP), :]
     for d in FAR_FIRST:
         ax_copy(d, 0).start()
         az_copy(d, 0).start()
-    att_xa[rows_a, :] = att_out_a[...]
+    att_xa[rows_a, :] = att_out_a[:PAIR, :]
     att_za[z] = att_out_a[...]
-    merged = merge([rows_b, rows_c], 1, pl.ds(PAIR, PAIR + GROUP * SAMP)).T.astype(BF16)
-    samples[...] = merged[PAIR:]
-    att_out_b[:PAIR, :] = merged[:PAIR]
-    att_out_b[PAIR:, :] = samples[pl.ds(pl.multiple_of(x * 2 * SAMP, 2 * SAMP), 2 * SAMP), :]
+    att_out_b[...] = merge([rows_b], 1, pl.ds(PAIR + GROUP * SAMP, PAIR)).T.astype(BF16)
     for d in FAR_FIRST:
         ax_copy(d, 1).start()
         az_copy(d, 1).start()
-    att_xb[rows_a, :] = att_out_b[:PAIR, :]
+    att_xb[rows_a, :] = att_out_b[...]
     att_zb[z] = att_out_b[...]
 
     def sum_z_copy(d, part):
@@ -528,23 +535,23 @@
     for d in (1, 2, 3):
         ax_copy(d, 0).wait()
         az_copy(d, 0).wait()
-    early_x = jnp.concatenate([att_xa[h * SPAN:(h + 1) * SPAN, :] for h in range(GROUP)], axis=1)
-    early_z = line_up(att_za, 0, SPAN)
+    early_x = jnp.concatenate(
+        [
+            jnp.concatenate([att_xa[h * SPAN:(h + 1) * SPAN, :] for h in range(GROUP)], axis=1),
+            jnp.concatenate([samples[h * SAMP:(h + 1) * SAMP, :] for h in range(GROUP)], axis=1),
+        ],
+        axis=0)
+    early_z = jnp.concatenate([line_up(att_za, 0, SPAN), line_up(att_za, PAIR, SAMP)], axis=0)
     project(0, early_x, early_z)
     for d in (1, 2, 3):
         ax_copy(d, 1).wait()
         az_copy(d, 1).wait()
-    late_x = jnp.concatenate(
-        [
-            jnp.concatenate([att_xb[h * SPAN:(h + 1) * SPAN, :] for h in range(GROUP)], axis=1),
-            jnp.concatenate([samples[h * SAMP:(h + 1) * SAMP, :] for h in range(GROUP)], axis=1),
-        ],
-        axis=0)
-    late_z = jnp.concatenate([line_up(att_zb, 0, SPAN), line_up(att_zb, PAIR, SAMP)], axis=0)
+    late_x = jnp.concatenate([att_xb[h * SPAN:(h + 1) * SPAN, :] for h in range(GROUP)], axis=1)
+    late_z = line_up(att_zb, 0, SPAN)
     project(1, late_x, late_z)
     sums_z = [jnp.dot(one, wout_x[z], preferred_element_type=F32) for one in (early_x, late_x)]
     sums_x = [jnp.dot(one, wout_z[x], preferred_element_type=F32) for one in (early_z, late_z)]
-    for part, rows in ((0, slice(0, SPAN)), (1, slice(SPAN, ROWS))):
+    for part in range(2):
         sum_x, sum_z = sums_x[part], sums_z[part]
         in_x, in_z = ((sum_in_xa, sum_in_za), (sum_in_xb, sum_in_zb))[part]
         for d in (1, 2, 3):
@@ -552,8 +559,12 @@
             sum_z = sum_z + in_z[d].astype(F32)
             sum_x_copy(d, part).wait()
             sum_x = sum_x + in_x[d].astype(F32)
-        out_ref[rows, :HALF] = sum_z.astype(BF16)
-        out_ref[rows, HALF:] = sum_x.astype(BF16)
+        for total, cols in ((sum_z, slice(0, HALF)), (sum_x, slice(HALF, OUT))):
+            if part == 0:
+                out_ref[:SPAN, cols] = total[:SPAN].astype(BF16)
+                out_ref[2 * SPAN:, cols] = total[SPAN:].astype(BF16)
+            else:
+                out_ref[SPAN:2 * SPAN, cols] = total.astype(BF16)
 
     for d in (1, 2, 3):
         slot_copy(d).wait_send()
@@ -578,16 +589,18 @@
 
 def local(hidden_in, norm_gain, w_query, w_keyval, w_out, kv_store, page_slots, page_counts):
     vmem = pl.BlockSpec(memory_space=pltpu.VMEM)
-    smem = pl.BlockSpec(memory_space=pltpu.SMEM)
     anywhere = pl.BlockSpec(memory_space=pl.ANY)
     dma = pltpu.SemaphoreType.DMA
-    slots = page_slots[:, 0, :]
+    slots = page_slots.transpose(2, 1, 0)
     return pl.pallas_call(
         layer_kernel,
-        out_shape=jax.ShapeDtypeStruct((ROWS, OUT), BF16),
-        in_specs=[vmem, smem, vmem, anywhere, anywhere, anywhere, anywhere, anywhere],
+        out_shape=pltpu.VMEM((ROWS, OUT), BF16),
+        in_specs=[anywhere, anywhere, anywhere, anywhere, anywhere, anywhere, anywhere, anywhere],
         out_specs=vmem,
         scratch_shapes=[
+            pltpu.SMEM((1, 128), jnp.int32),
+            pltpu.VMEM((1, D), F32),
+            pltpu.VMEM((CAP, 1, 8), jnp.int32),
             pltpu.VMEM((ROWS, D), BF16),
             pltpu.VMEM((D, 256), BF16),
             pltpu.VMEM((64, D), BF16),
@@ -618,30 +631,30 @@
             pltpu.VMEM((HD, 2 * PAIR + 128), F32),
             pltpu.VMEM((1, 2 * PAIR + 128), F32),
             pltpu.VMEM((1, 2 * PAIR + 128), F32),
+            pltpu.VMEM((4, HD, PAIR + 128), BF16),
+            pltpu.VMEM((4, HD, PAIR + 128), BF16),
+            pltpu.VMEM((4, 2, PAIR + 128), F32),
+            pltpu.VMEM((4, 2, PAIR + 128), F32),
             pltpu.VMEM((4, HD, PAIR), BF16),
             pltpu.VMEM((4, HD, PAIR), BF16),
-            pltpu.VMEM((4, 8, PAIR), F32),
-            pltpu.VMEM((4, 8, PAIR), F32),
-            pltpu.VMEM((4, HD, PAIR + 128), BF16),
-            pltpu.VMEM((4, HD, PAIR + 128), BF16),
-            pltpu.VMEM((4, 8, PAIR + 128), F32),
-            pltpu.VMEM((4, 8, PAIR + 128), F32),
+            pltpu.VMEM((4, 2, PAIR), F32),
+            pltpu.VMEM((4, 2, PAIR), F32),
+            pltpu.VMEM((PAIR + 2 * SAMP, HD), BF16),
             pltpu.VMEM((PAIR, HD), BF16),
-            pltpu.VMEM((PAIR + 2 * SAMP, HD), BF16),
             pltpu.VMEM((GROUP * SAMP, HD), BF16),
             pltpu.VMEM((4 * PAIR, HD), BF16),
             pltpu.VMEM((4 * PAIR, HD), BF16),
+            pltpu.VMEM((4, PAIR + 2 * SAMP, HD), BF16),
             pltpu.VMEM((4, PAIR, HD), BF16),
-            pltpu.VMEM((4, PAIR + 2 * SAMP, HD), BF16),
+            pltpu.VMEM((4, EARLY, HALF), BF16),
+            pltpu.VMEM((4, EARLY, HALF), BF16),
             pltpu.VMEM((4, SPAN, HALF), BF16),
             pltpu.VMEM((4, SPAN, HALF), BF16),
-            pltpu.VMEM((4, LATE, HALF), BF16),
-            pltpu.VMEM((4, LATE, HALF), BF16),
+            pltpu.VMEM((4, EARLY, HALF), BF16),
+            pltpu.VMEM((4, EARLY, HALF), BF16),
             pltpu.VMEM((4, SPAN, HALF), BF16),
             pltpu.VMEM((4, SPAN, HALF), BF16),
-            pltpu.VMEM((4, LATE, HALF), BF16),
-            pltpu.VMEM((4, LATE, HALF), BF16),
-            dma((4,)), dma((4,)), dma((4,)),
+            dma((7,)), dma((4,)), dma((4,)),
             dma((4,)), dma((4,)), dma((4,)), dma((4,)), dma((4,)), dma((4,)),
             dma((5 * SOURCES,)), dma((5 * SOURCES,)),
             dma((12,)), dma((12,)), dma((8,)), dma((8,)), dma((8,)), dma((8,)),
@@ -654,7 +667,7 @@
         cost_estimate=pl.CostEstimate(flops=17 * 10**9, bytes_accessed=19 * 10**6, transcendentals=27 * 10**6),
         name="layer",
     )(
-        slots, page_counts.reshape(-1), norm_gain.reshape(1, D), hidden_in, w_query, w_keyval.T, w_out,
+        slots, page_counts, norm_gain.reshape(1, D), hidden_in, w_query, w_keyval.T, w_out,
         kv_store.reshape(16, 4, 2 * PAGE, HD))
 
 

time: 115 us -> 110 us (0.957)
  local copies, waits for them, and re-layouts: 3.03 us -> 0.71 us
    pallas_call x1, Pallas kernels: 111 us -> 110 us  [local(): pl.pallas_call(layer_kernel, out_shape=pltpu.VMEM((ROWS, OUT), BF16), in_...]
    squeeze x1 -> x0, local copies, waits for them, and re-layouts: 1.35 us -> none  [local(): slots = page_slots[:, 0, :]]
where the time goes in v5:
time: 110 us
  Pallas kernels  110 us (100%)
    pallas_call x1, Pallas kernels, local(): pl.pallas_call(layer_kernel, out_shape=pltpu.VMEM((ROWS, OUT), BF16), in_...  110 us

profile of v5, /device:TPU:1, one launch (start us, length us, event | category | flops | bytes accessed | tf_op | source)
XLA Modules:
  0.0 110.3 jit_solution(2922549888217528930)
XLA Ops:
  0.0 109.6 %layer.1 = bf16[272,512]{1,0:T(8,128)(2,1)S(1)} custom-call(s32[3,1,8]{2,1,0:T(1,128)} %bitcast.7, s32[1,128]{1,0:T(1,128)} %counts_hbm.1, f32[1,8192]{1,0:T(1,128)} %bitcast.6, bf16[272,8192]{1,0:T(8,128)(2,1)} %hidden_hbm.1, bf16[8192,256]{1,0:T(8,128)(2,1)} %wq_hbm.1, bf16[64,8192]{1,0:T(8,128)(2,1)} %bitcast.5, bf16[256,8192]{1,0:T(8,128)(2,1)} %wout_hbm.1, ...), custom_call_target="tpu_custom_call" | custom-call | flops 16999999488 | bytes 19000000 | tf_op jit(solution)/shard_map/layer/pallas_call | solution.py:595
  109.6 0.7 copy.10

commit v6 on v5

--- a/solution.py
+++ b/solution.py
@@ -30,8 +30,8 @@
 SOURCES = 8
 EARLY_CHUNK = 4
 LAST_CHUNK = 2
-EARLY_STEPS = 3 * SOURCES // EARLY_CHUNK
-LAST_STEPS = SOURCES // LAST_CHUNK
+EARLY_STEPS = 7
+LAST_STEPS = 2
 HALF = 256
 PART = 512
 OUT = 512
@@ -261,6 +261,7 @@
         return remote(wout_z.at[part], wout_z.at[part], zw_s.at[n], zw_r.at[n], (y * 2 + 1 - c, tp))
 
     acc[...] = jnp.zeros_like(acc)
+    vt[HD:, :] = jnp.ones_like(vt[HD:, :])
     stat_m[...] = jnp.full_like(stat_m, -DEAD)
     stat_l[...] = jnp.zeros_like(stat_l)
 
@@ -357,7 +358,7 @@
         pages = yrecv[k, pl.ds(first, chunk)]
         keys = pages[:, :, :PAGE, :].reshape(slots * PAGE, HD)
         width = pl.ds(0, slots * PAGE)
-        vt[:, width] = pages[:, :, PAGE:, :].reshape(slots * PAGE, HD).T
+        vt[:HD, width] = pages[:, :, PAGE:, :].reshape(slots * PAGE, HD).T
 
         def some(tiles):
             cols = [pl.ds(t * TILE, TILE) for t in tiles]
@@ -370,17 +371,15 @@
                     new_m = jnp.maximum(new_m, jnp.where(live[j], top, -DEAD))
                 shift = new_m * scale
                 shrink = jnp.exp2(old_m * scale - shift)
-                total = stat_l[:, own] * shrink
                 weights = []
                 for j in range(slots):
                     probs = jnp.exp2(scores[j * PAGE:(j + 1) * PAGE] * scale - jnp.where(live[j], shift, DEAD))
-                    total = total + jnp.sum(probs, axis=0, keepdims=True)
                     weights.append(probs.astype(BF16))
                 blended = lax.dot_general(
                     vt[:, width], jnp.concatenate(weights, axis=0), NN, preferred_element_type=F32)
-                acc[:, own] = acc[:, own] * shrink + blended
+                acc[:, own] = acc[:, own] * shrink + blended[:HD]
                 stat_m[:, own] = new_m
-                stat_l[:, own] = total
+                stat_l[:, own] = stat_l[:, own] * shrink + blended[HD:HD + 1]
 
         some(FIRST_TILES)
         if between is not None:
@@ -427,18 +426,7 @@
                 for m in range(2):
                     wout_z_copy(d, m).start()
 
-        return carry
-
-    def last_step(n, carry):
-        def when_last(part):
-            @pl.when(n == LAST_STEPS - 1)
-            def _():
-                send_part(part)
-
-        attend(3, n * LAST_CHUNK, LAST_CHUNK, lambda: when_last(0))
-        when_last(1)
-
-        @pl.when(n == 0)
+        @pl.when(n == 5)
         def _():
             for m in range(2):
                 for d in (1, 2, 3):
@@ -446,13 +434,24 @@
                 own_wout_x(m).wait()
                 wout_x_share(m).start()
 
-        @pl.when(n == 1)
+        @pl.when(n == 6)
         def _():
             for m in range(2):
                 for d in (1, 2, 3):
                     wout_z_copy(d, m).wait()
                 own_wout_z(m).wait()
                 wout_z_share(m).start()
+
+        return carry
+
+    def last_step(n, carry):
+        def when_last(part):
+            @pl.when(n == LAST_STEPS - 1)
+            def _():
+                send_part(part)
+
+        attend(3, EARLY_CHUNK + n * LAST_CHUNK, LAST_CHUNK, lambda: when_last(0))
+        when_last(1)
 
         return carry
 
@@ -627,7 +626,7 @@
             pltpu.VMEM((HD, QPAD), F32),
             pltpu.VMEM((1, QPAD), F32),
             pltpu.VMEM((1, QPAD), F32),
-            pltpu.VMEM((HD, EARLY_CHUNK * CAP * PAGE), BF16),
+            pltpu.VMEM((HD + 16, EARLY_CHUNK * CAP * PAGE), BF16),
             pltpu.VMEM((HD, 2 * PAIR + 128), F32),
             pltpu.VMEM((1, 2 * PAIR + 128), F32),
             pltpu.VMEM((1, 2 * PAIR + 128), F32),

time: 110 us -> 110 us (level)
  no operation moved by 1% of the time
where the time goes in v6:
time: 110 us
  Pallas kernels  109 us (99%)
    pallas_call x1, Pallas kernels, local(): pl.pallas_call(layer_kernel, out_shape=pltpu.VMEM((ROWS, OUT), BF16), in_...  109 us

profile of v6, /device:TPU:1, one launch (start us, length us, event | category | flops | bytes accessed | tf_op | source)
XLA Modules:
  0.0 109.6 jit_solution(12303581407994616571)
XLA Ops:
  0.0 108.8 %layer.1 = bf16[272,512]{1,0:T(8,128)(2,1)S(1)} custom-call(s32[3,1,8]{2,1,0:T(1,128)} %bitcast.7, s32[1,128]{1,0:T(1,128)} %counts_hbm.1, f32[1,8192]{1,0:T(1,128)} %bitcast.6, bf16[272,8192]{1,0:T(8,128)(2,1)} %hidden_hbm.1, bf16[8192,256]{1,0:T(8,128)(2,1)} %wq_hbm.1, bf16[64,8192]{1,0:T(8,128)(2,1)} %bitcast.5, bf16[256,8192]{1,0:T(8,128)(2,1)} %wout_hbm.1, ...), custom_call_target="tpu_custom_call" | custom-call | flops 16999999488 | bytes 19000000 | tf_op jit(solution)/shard_map/layer/pallas_call | solution.py:594
  108.8 0.7 copy.10

commit v7 on v6

--- a/solution.py
+++ b/solution.py
@@ -172,8 +172,7 @@
     def _(n):
         part = hidden[:, pl.ds(pl.multiple_of(n * PART, PART), PART)].astype(F32)
         part = part * part
-        for m in range(PART // 128):
-            squares[...] += part[:, m * 128:(m + 1) * 128]
+        squares[...] += (part[:, :128] + part[:, 128:256]) + (part[:, 256:384] + part[:, 384:])
 
     half_copy(1).start()
     mean = jnp.sum(squares[...], axis=1, keepdims=True) * (1.0 / D)
@@ -519,10 +518,10 @@
     def project(part, attended_x, attended_z):
         out_x, out_z = ((sum_out_xa, sum_out_za), (sum_out_xb, sum_out_zb))[part]
         for d in FAR_FIRST:
+            out_x[d] = jnp.dot(attended_z, wout_z[(x + d) % 4], preferred_element_type=F32).astype(BF16)
+            sum_x_copy(d, part).start()
             out_z[d] = jnp.dot(attended_x, wout_x[(z + d) % 4], preferred_element_type=F32).astype(BF16)
             sum_z_copy(d, part).start()
-            out_x[d] = jnp.dot(attended_z, wout_z[(x + d) % 4], preferred_element_type=F32).astype(BF16)
-            sum_x_copy(d, part).start()
 
     def line_up(ref, start, size):
         return jnp.concatenate(

time: 110 us -> 110 us (level)
  no operation moved by 1% of the time
where the time goes in v7:
time: 110 us
  Pallas kernels  109 us (99%)
    pallas_call x1, Pallas kernels, local(): pl.pallas_call(layer_kernel, out_shape=pltpu.VMEM((ROWS, OUT), BF16), in_...  109 us

profile of v7, /device:TPU:1, one launch (start us, length us, event | category | flops | bytes accessed | tf_op | source)
XLA Modules:
  0.0 109.6 jit_solution(17064012232172501283)
XLA Ops:
  0.0 108.9 %layer.1 = bf16[272,512]{1,0:T(8,128)(2,1)S(1)} custom-call(s32[3,1,8]{2,1,0:T(1,128)} %bitcast.7, s32[1,128]{1,0:T(1,128)} %counts_hbm.1, f32[1,8192]{1,0:T(1,128)} %bitcast.6, bf16[272,8192]{1,0:T(8,128)(2,1)} %hidden_hbm.1, bf16[8192,256]{1,0:T(8,128)(2,1)} %wq_hbm.1, bf16[64,8192]{1,0:T(8,128)(2,1)} %bitcast.5, bf16[256,8192]{1,0:T(8,128)(2,1)} %wout_hbm.1, ...), custom_call_target="tpu_custom_call" | custom-call | flops 16999999488 | bytes 19000000 | tf_op jit(solution)/shard_map/layer/pallas_call | solution.py:593
  108.9 0.7 copy.10
